TPU v7x, 32 devices: a whole 2x2x4 slice. The times are simulated.
32 devices in a mesh: node: 8 (over z, y), local: 4 (over x, core).
Axes of the slice: x: 2, y: 2, z: 4, core: 2. Of those that a mesh axis runs over, the one named last changes fastest.
Arguments:
- activations: bfloat16 [8192, 5120], P(('node', 'local')), may hold values from -6 to 6
- queries: bfloat16 [8192, 5120], P(('node', 'local')), may hold values from -100 to 100
- rotated_key_value: bfloat16 [8192, 2048], P(('node', 'local')), may hold values from -5 to 5
- attention_out_grad: bfloat16 [8192, 5120], P(('node', 'local')), may hold values from -6 to 6
- adapter_down: bfloat16 [5120, 128], replicated, may hold values from -0.078125 to 0.078125
- adapter_up: bfloat16 [128, 1024], replicated, may hold values from -0.75 to 0.75
- bin_local_index: int32 [32, 256], P(('node', 'local')), may hold values from 0 to 3, as said below
- bin_row_offset: int32 [32, 256], P(('node', 'local')), may hold values from 0 to 3, as said below
- spill_node: int32 [32, 256], P(('node', 'local')), may hold values from 0 to 7, as said below
- spill_row_offset: int32 [32, 256], P(('node', 'local')), may hold values from 0 to 3, as said below
- arrival_pick_index: int32 [32, 256], P(('node', 'local')), may hold values from 0 to 303, as said below
- packed_sequence_number: int32 [32, 256], P(('node', 'local')), may hold values from 0 to 7, never falling along the last dimension, each value on 1 to 128 neighbouring positions
Outputs:
- key_value_cotangent: bfloat16 [8192, 2048], P(('node', 'local'))
- down_factor_grad: float32 [5120, 128], P(('node', 'local'))
- up_factor_grad_transposed: float32 [1024, 128], P(('node', 'local'))
Inputs may be any that keep to these rules, and one draw needn't show every extreme that they name: `bin_local_index`: rows that stay or overflow carry the device's own local index. At most 4 rows of a device go to one other bin of its node, and that bin sends back exactly as many to it; in every node one device sends 4 rows to every other bin of the node. `bin_row_offset`: offsets of the rows one device sends to one bin are 0 up to their count minus 1; zero for other rows. `spill_node`: A row moves across nodes only if it stays in its node's bin of its own local index otherwise; at most 4 rows of a device go to one other node, and as many come back; for every local index one node sends 4 rows to every other node. Rows that do not overflow carry their own node. `spill_row_offset`: offsets of the overflow rows one device sends to one node are 0 up to their count minus 1; zero for other rows. `arrival_pick_index`: every bin holds exactly 256 rows: each row of the arrival list of 304 entries that is filled is named once, and no empty entry is named.
All inputs are finite; a program needn't handle non-finite values.
Results may differ from a plain program's by a relative error of at most 0.0056.
Values may be sent and summed in bfloat16 or wider, within the bound.
A program may use at most 128 MiB of HBM per device.

v0:
```python
import math

import jax
import jax.numpy as jnp
from jax import lax
from jax.sharding import PartitionSpec as P

KV_HEADS = 8
HEAD = 128
ADAPTER_RANK = 64
CAP_L = 4
CAP_N = 4
GROUP = 5
KEY_HEAD_WIDTH = 1024


rope_theta = 1000000.0


def rope_tables(segments):
    slot_ids = jnp.arange(segments.shape[0], dtype=jnp.int32)
    seg_start = jnp.sum((segments[None, :] < segments[:, None]).astype(jnp.int32), axis=1)
    position = (slot_ids - seg_start).astype(jnp.float32)
    frequency = rope_theta ** (-jnp.arange(0, HEAD, 2).astype(jnp.float32) / HEAD)
    angles = position[:, None] * frequency[None, :]
    return (jnp.cos(angles), jnp.sin(angles))


def unrotate(key_rot, cosine_table, sine_table):
    half_head = HEAD // 2
    first_half = key_rot[..., :half_head]
    second_half = key_rot[..., half_head:]
    cos_rows = cosine_table[:, None, :]
    sin_rows = sine_table[:, None, :]
    return jnp.concatenate(
        [
            first_half * cos_rows + second_half * sin_rows,
            second_half * cos_rows - first_half * sin_rows,
        ],
        axis=-1,
    )


def attention_backward(query_rows, kv_rows, grad_rows, segments):
    row_count = query_rows.shape[0]
    score_scale = 1.0 / math.sqrt(HEAD)
    slot_ids = jnp.arange(row_count, dtype=jnp.int32)
    allowed = (segments[:, None] == segments[None, :]) & (slot_ids[None, :] <= slot_ids[:, None])
    query_groups = query_rows.reshape(row_count, KV_HEADS, GROUP * HEAD)
    grad_groups = grad_rows.reshape(row_count, KV_HEADS, GROUP * HEAD)
    key_heads = kv_rows[:, :KEY_HEAD_WIDTH].reshape(row_count, KV_HEADS, HEAD)
    value_heads = kv_rows[:, KEY_HEAD_WIDTH:].reshape(row_count, KV_HEADS, HEAD)

    def per_group(group_id):
        query_block = lax.dynamic_index_in_dim(query_groups, group_id, 1, keepdims=False).reshape(
            row_count, GROUP, HEAD
        )
        grad_block = lax.dynamic_index_in_dim(grad_groups, group_id, 1, keepdims=False).reshape(
            row_count, GROUP, HEAD
        )
        key_block = lax.dynamic_index_in_dim(key_heads, group_id, 1, keepdims=False)
        value_block = lax.dynamic_index_in_dim(value_heads, group_id, 1, keepdims=False)
        scores = (
            jnp.einsum("isd,jd->sij", query_block, key_block, preferred_element_type=jnp.float32)
            * score_scale
        )
        scores = jnp.where(allowed[None], scores, -jnp.inf)
        row_max = jnp.max(scores, axis=-1, keepdims=True)
        weights = jnp.exp(scores - row_max)
        probs = weights / jnp.sum(weights, axis=-1, keepdims=True)
        prob_grad = jnp.einsum(
            "isd,jd->sij", grad_block, value_block, preferred_element_type=jnp.float32
        )
        row_delta = jnp.sum(probs * prob_grad, axis=-1, keepdims=True)
        score_grad = (probs * (prob_grad - row_delta)).astype(jnp.bfloat16)
        value_cotangent_rows = jnp.einsum(
            "sij,isd->jd",
            probs.astype(jnp.bfloat16),
            grad_block,
            preferred_element_type=jnp.float32,
        )
        key_rot = (
            jnp.einsum("sij,isd->jd", score_grad, query_block, preferred_element_type=jnp.float32)
            * score_scale
        )
        return (key_rot, value_cotangent_rows)

    key_rot, value_cotangent_rows = lax.map(per_group, jnp.arange(KV_HEADS, dtype=jnp.int32))
    key_rot = jnp.transpose(key_rot, (1, 0, 2))
    value_cotangent_rows = jnp.transpose(value_cotangent_rows, (1, 0, 2))
    cosine_table, sine_table = rope_tables(segments)
    key_cotangent_rows = unrotate(key_rot, cosine_table, sine_table)
    return jnp.concatenate(
        [
            key_cotangent_rows.reshape(row_count, KEY_HEAD_WIDTH),
            value_cotangent_rows.reshape(row_count, KEY_HEAD_WIDTH),
        ],
        axis=1,
    ).astype(jnp.bfloat16)


def adapter_terms(active_rows, key_value_cotangent, adapter_down, adapter_up):
    key_cotangent_rows = key_value_cotangent[:, :KEY_HEAD_WIDTH]
    value_cotangent_rows = key_value_cotangent[:, KEY_HEAD_WIDTH:]
    raise_key = jnp.dot(
        key_cotangent_rows, adapter_up[:ADAPTER_RANK].T, preferred_element_type=jnp.float32
    )
    raise_value = jnp.dot(
        value_cotangent_rows, adapter_up[ADAPTER_RANK:].T, preferred_element_type=jnp.float32
    )
    lift = jnp.concatenate([raise_key, raise_value], axis=1).astype(jnp.bfloat16)
    down_factor_grad = jnp.dot(active_rows.T, lift, preferred_element_type=jnp.float32)
    down_product = jnp.dot(active_rows, adapter_down, preferred_element_type=jnp.float32).astype(
        jnp.bfloat16
    )
    up_key = jnp.dot(
        key_cotangent_rows.T, down_product[:, :ADAPTER_RANK], preferred_element_type=jnp.float32
    )
    up_value = jnp.dot(
        value_cotangent_rows.T, down_product[:, ADAPTER_RANK:], preferred_element_type=jnp.float32
    )
    return (down_factor_grad, jnp.concatenate([up_key, up_value], axis=1))


def pack_rows(source_rows, slot_ids, capacity):
    empty_rows = jnp.zeros((capacity, source_rows.shape[1]), source_rows.dtype)
    return empty_rows.at[slot_ids].set(source_rows, mode="drop")


def local(
    activations,
    queries,
    rotated_key_value,
    attention_out_grad,
    adapter_down,
    adapter_up,
    bin_local_index,
    bin_row_offset,
    spill_node,
    spill_row_offset,
    arrival_pick_index,
    packed_sequence_number,
):
    row_count = activations.shape[0]
    local_count = lax.axis_size("local")
    node_count = lax.axis_size("node")
    near_total = local_count * CAP_L
    far_total = node_count * CAP_N
    own_local = lax.axis_index("local")
    own_node = lax.axis_index("node")
    bin_local_index = bin_local_index.reshape(-1)
    bin_row_offset = bin_row_offset.reshape(-1)
    spill_node = spill_node.reshape(-1)
    spill_row_offset = spill_row_offset.reshape(-1)
    arrival_pick_index = arrival_pick_index.reshape(-1)
    segments = packed_sequence_number.reshape(-1)
    moved_in = bin_local_index != own_local
    moved_out = spill_node != own_node
    local_slots = jnp.where(moved_in, bin_local_index * CAP_L + bin_row_offset, near_total)
    node_slots = jnp.where(moved_out, spill_node * CAP_N + spill_row_offset, far_total)

    def assemble(own_rows, near_rows, far_rows):
        arrivals = jnp.concatenate([own_rows, near_rows, far_rows], axis=0)
        return jnp.take(arrivals, arrival_pick_index, axis=0)

    near_rows = (
        lax.all_to_all(
            pack_rows(activations, local_slots, near_total),
            "local",
            split_axis=0,
            concat_axis=0,
            tiled=True,
        ),
        lax.all_to_all(
            pack_rows(queries, local_slots, near_total),
            "local",
            split_axis=0,
            concat_axis=0,
            tiled=True,
        ),
        lax.all_to_all(
            pack_rows(rotated_key_value, local_slots, near_total),
            "local",
            split_axis=0,
            concat_axis=0,
            tiled=True,
        ),
        lax.all_to_all(
            pack_rows(attention_out_grad, local_slots, near_total),
            "local",
            split_axis=0,
            concat_axis=0,
            tiled=True,
        ),
    )
    far_rows = (
        lax.all_to_all(
            pack_rows(activations, node_slots, far_total),
            "node",
            split_axis=0,
            concat_axis=0,
            tiled=True,
        ),
        lax.all_to_all(
            pack_rows(queries, node_slots, far_total),
            "node",
            split_axis=0,
            concat_axis=0,
            tiled=True,
        ),
        lax.all_to_all(
            pack_rows(rotated_key_value, node_slots, far_total),
            "node",
            split_axis=0,
            concat_axis=0,
            tiled=True,
        ),
        lax.all_to_all(
            pack_rows(attention_out_grad, node_slots, far_total),
            "node",
            split_axis=0,
            concat_axis=0,
            tiled=True,
        ),
    )
    active_bin = assemble(activations, near_rows[0], far_rows[0])
    query_bin = assemble(queries, near_rows[1], far_rows[1])
    kv_bin = assemble(rotated_key_value, near_rows[2], far_rows[2])
    grad_bin = assemble(attention_out_grad, near_rows[3], far_rows[3])
    key_value_cotangent = attention_backward(query_bin, kv_bin, grad_bin, segments)
    down_factor_grad, up_factor_grad_transposed = adapter_terms(
        active_bin, key_value_cotangent, adapter_down, adapter_up
    )
    totals = (
        lax.psum_scatter(down_factor_grad, ("node", "local"), scatter_dimension=0, tiled=True),
        lax.psum_scatter(
            up_factor_grad_transposed, ("node", "local"), scatter_dimension=0, tiled=True
        ),
    )
    factor = 1.0 / math.sqrt(row_count * local_count * node_count)
    return (key_value_cotangent, totals[0] * factor, totals[1] * factor)


def solution(mesh):
    placed = (
        P(("node", "local"), None),
        P(("node", "local"), None),
        P(("node", "local"), None),
        P(("node", "local"), None),
        P(),
        P(),
        P(("node", "local"), None),
        P(("node", "local"), None),
        P(("node", "local"), None),
        P(("node", "local"), None),
        P(("node", "local"), None),
        P(("node", "local"), None),
    )
    return jax.shard_map(
        local,
        mesh=mesh,
        in_specs=placed,
        out_specs=(
            P(("node", "local"), None),
            P(("node", "local"), None),
            P(("node", "local"), None),
        ),
        check_vma=False,
    )
```

profile of v0, /device:TPU:0, one launch (start us, length us, event | category | flops | bytes accessed | tf_op | source)
XLA Modules:
  0.0 531.4 jit_solution(11561637572019909105)
XLA Ops:
  8.0 2.7 scatter_custom_fusion
  11.3 4.2 all-to-all-start
  18.5 5.0 scatter_custom_fusion.2
  24.3 5.0 scatter_custom_fusion.4
  30.1 3.3 all-to-all-start.2
  33.5 4.9 all-to-all-done.2
  38.4 3.8 all-to-all-start.4
  42.9 5.0 scatter_custom_fusion.6
  48.7 3.4 all-to-all-start.6
  52.1 5.1 scatter_custom_fusion.3
  57.2 5.3 scatter_custom_fusion.5
  62.5 2.7 scatter_custom_fusion.1
  65.2 5.1 scatter_custom_fusion.7
  73.6 6.4 %all-to-all-start.1 = ((bf16[8,4,2048]{2,1,0:T(4,128)(2,1)}), bf16[8,4,2048]{2,1,0:T(4,128)(2,1)S(1)}, u32[]{:S(2)}, u32[]{:S(2)}) async-start(bf16[8,4,2048]{2,1,0:T(4,128)(2,1)} %all_to_all.67), calls=%async_computation.1 | async-start | bytes 262144 | tf_op jit(solution)/shard_map/all_to_all | solution.py:211
  82.0 5.6 %all-to-all-done.1 = bf16[8,4,2048]{2,1,0:T(4,128)(2,1)S(1)} async-done(((bf16[8,4,2048]{2,1,0:T(4,128)(2,1)}), bf16[8,4,2048]{2,1,0:T(4,128)(2,1)S(1)}, u32[]{:S(2)}, u32[]{:S(2)}) %all-to-all-start.1) | async-done | bytes 131104 | tf_op jit(solution)/shard_map/all_to_all | solution.py:211
  87.6 3.4 all-to-all-start.3
  97.5 3.1 all-to-all-done.3
  100.6 3.6 all-to-all-start.5
  104.3 3.1 pad_maximum_fusion
  107.4 8.5 %gather_fusion.1 = bf16[256,5120]{1,0:T(8,128)(2,1)} fusion(bf16[304,5120]{1,0:T(8,128)(2,1)} %pad_maximum_fusion, s32[1024]{0:T(1024)S(1)} %pad_clamp_fusion), kind=kCustom, calls=%fused_computation.clone | custom fusion | bytes 5243904 | tf_op jit(solution)/shard_map/jit(_take)/gather | solution.py:164
  115.8 6.0 %all-to-all-start.7 = ((bf16[8,4,5120]{2,1,0:T(4,128)(2,1)}), bf16[8,4,5120]{2,1,0:T(4,128)(2,1)S(1)}, u32[]{:S(2)}, u32[]{:S(2)}) async-start(bf16[8,4,5120]{2,1,0:T(4,128)(2,1)} %all_to_all.85), calls=%async_computation.7 | async-start | bytes 655360 | tf_op jit(solution)/shard_map/all_to_all | solution.py:197
  122.2 3.1 pad_maximum_fusion.1
  125.3 8.5 %gather_fusion.2 = bf16[256,5120]{1,0:T(8,128)(2,1)} fusion(bf16[304,5120]{1,0:T(8,128)(2,1)} %pad_maximum_fusion.1, s32[1024]{0:T(1024)S(1)} %pad_clamp_fusion), kind=kCustom, calls=%fused_computation.1.clone | custom fusion | bytes 5243904 | tf_op jit(solution)/shard_map/jit(_take)/gather | solution.py:164
  133.8 5.4 %broadcast_select_fusion.1 = (bf16[256,5120]{1,0:T(8,128)(2,1)}, bf16[256,5120]{1,0:T(8,128)(2,1)}) fusion(bf16[256,5120]{1,0:T(8,128)(2,1)} %gather_fusion.2, pred[256]{0:T(512)(128)(4,1)S(1)} %compare_and_fusion, bf16[256,5120]{1,0:T(8,128)(2,1)} %gather_fusion.1), kind=kLoop, calls=%fused_computation.51 | loop fusion | flops 2621440 | bytes 10486016 | tf_op jit(solution)/shard_map/jit(_take)/select_n | solution.py:164
  139.2 4.4 copy.57
  143.6 4.5 copy.58
  148.0 86.1 %while.13 = (s32[]{:T(128)}, f32[8,256,128]{2,1,0:T(8,128)S(1)}, bf16[8,256,128]{2,1,0:T(8,128)(2,1)}, s32[8]{0:T(128)S(1)}, bf16[256,8,128]{2,0,1:T(8,128)(2,1)...) while((s32[]{:T(128)}, f32[8,256,128]{2,1,0:T(8,128)S(1)}, ...), condition=%wide.region_10.12_spmd.clone, body=%wide.region_6.11_spmd.clone.sunk | while | flops 340032512 | bytes 16315115 | solution.py:88
  151.8 3.1 fusion.90
  154.9 2.4 fusion.92
  162.6 3.1 fusion.90
  165.7 2.4 fusion.92
  173.4 3.1 fusion.90
  184.1 3.1 fusion.90
  187.2 2.4 fusion.92
  194.9 3.1 fusion.90
  197.9 2.4 fusion.92
  205.6 3.1 fusion.90
  208.7 2.4 fusion.92
  216.4 3.1 fusion.90
  219.5 2.4 fusion.92
  227.2 3.1 fusion.90
  230.2 2.4 fusion.92
  234.3 3.4 pad_maximum_fusion.2
  237.6 8.5 %gather_fusion.3 = bf16[256,5120]{1,0:T(8,128)(2,1)} fusion(bf16[304,5120]{1,0:T(8,128)(2,1)} %pad_maximum_fusion.2, s32[1024]{0:T(1024)S(1)} %pad_clamp_fusion), kind=kCustom, calls=%fused_computation.2.clone | custom fusion | bytes 5243904 | tf_op jit(solution)/shard_map/jit(_take)/gather | solution.py:164
  246.2 2.9 convolution_convert_fusion
  253.8 4.3 fusion.31
  259.5 127.0 %reduce-scatter.7.cloned.1.call-done = f32[32,128]{1,0:T(8,128)} async-done(((f32[1024,128]{1,0:T(8,128)}), f32[32,128]{1,0:T(8,128)}) %reduce-scatter.7.cloned.1.call-update) | async-done | bytes 16400
  388.0 134.7 %reduce-scatter.5.cloned.1.call-done = f32[160,128]{1,0:T(8,128)} async-done(((f32[5120,128]{1,0:T(8,128)}), f32[160,128]{1,0:T(8,128)}) %reduce-scatter.5.cloned.1.call-update) | async-done | bytes 81936 | tf_op jit(solution)/shard_map/reduce_scatter | solution.py:235
  (143 shorter events, 57.6 us)
Async XLA Ops:
  7.2 239.0 %copy-start = (bf16[5120,128]{1,0:T(8,128)(2,1)S(1)}, bf16[5120,128]{1,0:T(8,128)(2,1)}, u32[]{:S(2)}) copy-start(bf16[5120,128]{1,0:T(8,128)(2,1)} %param.20) | copy-start | bytes 3932164
  11.3 18.8 %all-to-all-start = ((bf16[4,4,2048]{2,1,0:T(4,128)(2,1)}), bf16[4,4,2048]{2,1,0:T(4,128)(2,1)S(1)}, u32[]{:S(2)}, u32[]{:S(2)}) async-start(bf16[4,4,2048]{2,1,0:T(4,128)(2,1)} %all_to_all.64), calls=%async_computation | async-start | bytes 131072 | tf_op jit(solution)/shard_map/all_to_all | solution.py:181
  30.1 8.3 %all-to-all-start.2 = ((bf16[4,4,5120]{2,1,0:T(4,128)(2,1)}), bf16[4,4,5120]{2,1,0:T(4,128)(2,1)S(1)}, u32[]{:S(2)}, u32[]{:S(2)}) async-start(bf16[4,4,5120]{2,1,0:T(4,128)(2,1)} %all_to_all.70), calls=%async_computation.2 | async-start | bytes 327680 | tf_op jit(solution)/shard_map/all_to_all | solution.py:174
  38.4 10.3 %all-to-all-start.4 = ((bf16[4,4,5120]{2,1,0:T(4,128)(2,1)}), bf16[4,4,5120]{2,1,0:T(4,128)(2,1)S(1)}, u32[]{:S(2)}, u32[]{:S(2)}) async-start(bf16[4,4,5120]{2,1,0:T(4,128)(2,1)} %all_to_all.76), calls=%async_computation.4 | async-start | bytes 327680 | tf_op jit(solution)/shard_map/all_to_all | solution.py:188
  48.7 24.9 %all-to-all-start.6 = ((bf16[4,4,5120]{2,1,0:T(4,128)(2,1)}), bf16[4,4,5120]{2,1,0:T(4,128)(2,1)S(1)}, u32[]{:S(2)}, u32[]{:S(2)}) async-start(bf16[4,4,5120]{2,1,0:T(4,128)(2,1)} %all_to_all.82), calls=%async_computation.6 | async-start | bytes 327680 | tf_op jit(solution)/shard_map/all_to_all | solution.py:167
  73.6 14.0 %all-to-all-start.1 = ((bf16[8,4,2048]{2,1,0:T(4,128)(2,1)}), bf16[8,4,2048]{2,1,0:T(4,128)(2,1)S(1)}, u32[]{:S(2)}, u32[]{:S(2)}) async-start(bf16[8,4,2048]{2,1,0:T(4,128)(2,1)} %all_to_all.67), calls=%async_computation.1 | async-start | bytes 262144 | tf_op jit(solution)/shard_map/all_to_all | solution.py:211
  87.6 13.0 %all-to-all-start.3 = ((bf16[8,4,5120]{2,1,0:T(4,128)(2,1)}), bf16[8,4,5120]{2,1,0:T(4,128)(2,1)S(1)}, u32[]{:S(2)}, u32[]{:S(2)}) async-start(bf16[8,4,5120]{2,1,0:T(4,128)(2,1)} %all_to_all.73), calls=%async_computation.3 | async-start | bytes 655360 | tf_op jit(solution)/shard_map/all_to_all | solution.py:204
  100.6 15.2 %all-to-all-start.5 = ((bf16[8,4,5120]{2,1,0:T(4,128)(2,1)}), bf16[8,4,5120]{2,1,0:T(4,128)(2,1)S(1)}, u32[]{:S(2)}, u32[]{:S(2)}) async-start(bf16[8,4,5120]{2,1,0:T(4,128)(2,1)} %all_to_all.79), calls=%async_computation.5 | async-start | bytes 655360 | tf_op jit(solution)/shard_map/all_to_all | solution.py:218
  115.8 118.3 %all-to-all-start.7 = ((bf16[8,4,5120]{2,1,0:T(4,128)(2,1)}), bf16[8,4,5120]{2,1,0:T(4,128)(2,1)S(1)}, u32[]{:S(2)}, u32[]{:S(2)}) async-start(bf16[8,4,5120]{2,1,0:T(4,128)(2,1)} %all_to_all.85), calls=%async_computation.7 | async-start | bytes 655360 | tf_op jit(solution)/shard_map/all_to_all | solution.py:197
  121.8 264.6 %reduce-scatter.7.cloned.1.call-start = ((), (), s32[]{:S(2)}) async-start(), calls=%async_computation.11 | async-start | bytes 540672
  143.6 4.5 copy-start.1
  143.6 4.5 copy-start.5
  154.9 2.4 copy-start.6
  154.9 2.4 copy-start.7
  165.7 2.4 copy-start.6
  165.7 2.4 copy-start.7
  176.4 2.4 copy-start.6
  176.4 2.4 copy-start.7
  187.2 2.4 copy-start.6
  187.2 2.4 copy-start.7
  197.9 2.4 copy-start.6
  197.9 2.4 copy-start.7
  208.7 2.4 copy-start.6
  208.7 2.4 copy-start.7
  219.5 2.4 copy-start.6
  219.5 2.4 copy-start.7
  230.2 2.4 copy-start.6
  230.2 2.4 copy-start.7
  246.2 2.9 copy-start.2
  246.2 3.1 copy-start.4
  249.7 2.9 copy-start.3
  251.2 271.4 %reduce-scatter.5.cloned.1.call-start = ((), (), s32[]{:S(2)}) async-start(), calls=%async_computation.10 | async-start | bytes 2703360 | tf_op jit(solution)/shard_map/reduce_scatter | solution.py:235
Sparse Core Ops, SparseCore 0:
  251.3 135.0 reduce-scatter.6
  388.8 133.7 reduce-scatter.4
where the time goes:
time: 541 us; the launch traced here: 531 us
  waiting for transfers between devices  275 us (51%)
  local copies, waits for them, and re-layouts  97.5 us (18%)
  matrix products  66 us (12%)
  starting transfers between devices  34.4 us (6%)
  other arithmetic  27.4 us (5%)
  loops' own time  15.9 us (3%)
  between operations  14.8 us (3%)
    reduce_scatter x1, waiting for transfers between devices, local(): lax.psum_scatter(down_factor_grad, ('node', 'local'), scatter_dimension=0...  135 us
    unnamed x3, waiting for transfers between devices  127 us
    scatter x8, local copies, waits for them, and re-layouts, pack_rows(): return empty_rows.at[slot_ids].set(source_rows, mode='drop')  36 us
    gather x4, local copies, waits for them, and re-layouts, assemble(): return jnp.take(arrivals, arrival_pick_index, axis=0)  27.8 us
    sub x8, matrix products, per_group(): weights = jnp.exp(scores - row_max)  24.5 us
    dot_general x8, matrix products, per_group(): jnp.einsum('sij,isd->jd', probs.astype(jnp.bfloat16), grad_block, preferr...  19.1 us
    another operation x1, loops' own time, attention_backward(): lax.map(per_group, jnp.arange(KV_HEADS, dtype=jnp.int32))  15.9 us
    unnamed x19, local copies, waits for them, and re-layouts  12.7 us
  transfers between devices with their start and end apart: 10, of which 5 were waited for; matrix products, arithmetic and copies ran while one was open for 30% of the time, Pallas kernels for 0%

commit v1 on v0

v1 whole, which is shorter than its diff:
```python
import functools
import math

import jax
import jax.numpy as jnp
import numpy as np
from jax import lax
from jax.experimental import pallas as pl
from jax.experimental.pallas import tpu as pltpu
from jax.sharding import PartitionSpec as P

KV_HEADS = 8
HEAD = 128
ADAPTER_RANK = 64
CAP = 4
GROUP = 5
KEY_HEAD_WIDTH = 1024
CHUNK = 16
GW = (2 * GROUP + 2) * HEAD
GQ = GW // 4
ROPE_THETA = 1000000.0
F32 = jnp.float32
BF16 = jnp.bfloat16


def dot(a, b):
    return jnp.dot(a, b, preferred_element_type=F32)


def dot_t(a, b):
    return lax.dot_general(a, b, (((1,), (1,)), ((), ())), preferred_element_type=F32)


def dot_l(a, b):
    return lax.dot_general(a, b, (((0,), (0,)), ((), ())), preferred_element_type=F32)


def iota(shape, axis):
    return lax.broadcasted_iota(jnp.int32, shape, axis)


def column(row):
    rows = row.shape[1]
    wide = jnp.broadcast_to(row.astype(F32), (128, rows))
    return jnp.transpose(wide)[:, 0:1].astype(jnp.int32)


def main_kernel(
    n_local,
    n_node,
    x_hbm,
    q_hbm,
    kv_hbm,
    g_hbm,
    down_hbm,
    up_ref,
    bl_ref,
    bo_ref,
    sn_ref,
    so_ref,
    pick_ref,
    seg_ref,
    cot_hbm,
    ddown_ref,
    dup_ref,
    stage,
    x_st,
    down_v,
    send,
    send_x,
    arr,
    arr_x,
    pack_hot,
    own_hot,
    arr_hot,
    bias,
    cos_v,
    sin_v,
    pk,
    xp,
    keys_out,
    vals_out,
    lift,
    load_sem,
    xload_sem,
    out_sem,
    send_sem,
    recv_sem,
):
    rows = x_st.shape[0]
    width = x_st.shape[1]
    xq = width // 4
    own_l = lax.axis_index("local")
    own_n = lax.axis_index("node")
    peers = n_local + n_node
    entries = peers * CHUNK

    def load(j):
        copies = []
        spans = (
            (q_hbm, j * (GROUP * HEAD), GROUP * HEAD, 0),
            (g_hbm, j * (GROUP * HEAD), GROUP * HEAD, GROUP * HEAD),
            (kv_hbm, j * HEAD, HEAD, 2 * GROUP * HEAD),
            (kv_hbm, KEY_HEAD_WIDTH + j * HEAD, HEAD, (2 * GROUP + 1) * HEAD),
        )
        for i, (src, at, size, to) in enumerate(spans):
            copies.append(
                pltpu.make_async_copy(
                    src.at[:, pl.ds(pl.multiple_of(at, HEAD), size)],
                    stage.at[j, :, to : to + size],
                    load_sem.at[j, i],
                )
            )
        return copies

    x_copy = pltpu.make_async_copy(x_hbm, x_st, xload_sem.at[0])
    down_copy = pltpu.make_async_copy(down_hbm, down_v, xload_sem.at[1])

    barrier = pltpu.get_barrier_semaphore()
    for o in range(1, n_local):
        pl.semaphore_signal(
            barrier,
            inc=1,
            device_id={"local": lax.rem(own_l + o, n_local)},
            device_id_type=pl.DeviceIdType.MESH,
        )
    for o in range(1, n_node):
        pl.semaphore_signal(
            barrier,
            inc=1,
            device_id={"node": lax.rem(own_n + o, n_node)},
            device_id_type=pl.DeviceIdType.MESH,
        )

    def start_load(j, c):
        for copy in load(j):
            copy.start()
        return c

    lax.fori_loop(0, KV_HEADS, start_load, 0)
    x_copy.start()
    down_copy.start()

    moved_in = bl_ref[...] != own_l
    moved_out = sn_ref[...] != own_n
    code = jnp.where(
        moved_in,
        bl_ref[...] * CAP + bo_ref[...],
        jnp.where(moved_out, (n_local + sn_ref[...]) * CAP + so_ref[...], -1),
    )
    a_sub = iota((entries, rows), 0)
    hit = code == (a_sub // CHUNK) * CAP + a_sub % CAP
    for c in range(4):
        pack_hot[c] = jnp.where(hit & ((a_sub // CAP) % 4 == c), 1.0, 0.0).astype(BF16)
    pick = column(pick_ref[...])
    own_hot[...] = jnp.where(pick == iota((rows, rows), 1), 1.0, 0.0).astype(BF16)
    a_lane = iota((rows, entries), 1)
    got = pick == rows + (a_lane // CHUNK) * CAP + a_lane % CAP
    for c in range(4):
        arr_hot[c] = jnp.where(got & ((a_lane // CAP) % 4 == c), 1.0, 0.0).astype(BF16)

    for slot in (own_l, n_local + own_n):
        arr_x[slot] = jnp.zeros(arr_x.shape[1:], BF16)

    def clear(j, c):
        for slot in (own_l, n_local + own_n):
            arr[j, slot] = jnp.zeros(arr.shape[2:], BF16)
        return c

    lax.fori_loop(0, KV_HEADS, clear, 0)

    pl.semaphore_wait(barrier, n_local - 1 + n_node - 1)

    def message(j, axis, o, src, dst):
        count, me, base = (n_local, own_l, 0) if axis == "local" else (n_node, own_n, n_local)
        to = lax.rem(me + o, count)
        return pltpu.make_async_remote_copy(
            src_ref=src.at[base + to],
            dst_ref=dst.at[base + me],
            send_sem=send_sem.at[j, base + to],
            recv_sem=recv_sem.at[j, base + me],
            device_id={axis: to},
            device_id_type=pl.DeviceIdType.MESH,
        )

    def arrival(j, axis, o, src, dst):
        count, me, base = (n_local, own_l, 0) if axis == "local" else (n_node, own_n, n_local)
        frm = lax.rem(me + count - o, count)
        return pltpu.make_async_remote_copy(
            src_ref=src.at[base + frm],
            dst_ref=dst.at[base + frm],
            send_sem=send_sem.at[j, base + frm],
            recv_sem=recv_sem.at[j, base + frm],
            device_id={axis: frm},
            device_id_type=pl.DeviceIdType.MESH,
        )

    hops = [("node", o) for o in range(1, n_node)] + [("local", o) for o in range(1, n_local)]

    def pack(j, carry):
        for copy in load(j):
            copy.wait()
        total = dot(pack_hot[0], stage[j, :, 0:GQ])
        for c in range(1, 4):
            total += dot(pack_hot[c], stage[j, :, c * GQ : (c + 1) * GQ])
        send[j] = total.astype(BF16).reshape(peers, CHUNK, GQ)
        for axis, o in hops:
            message(j, axis, o, send.at[j], arr.at[j]).start()
        return carry

    lax.fori_loop(0, KV_HEADS, pack, 0)
    x_copy.wait()
    total = dot(pack_hot[0], x_st[:, 0:xq])
    for c in range(1, 4):
        total += dot(pack_hot[c], x_st[:, c * xq : (c + 1) * xq])
    send_x[...] = total.astype(BF16).reshape(peers, CHUNK, xq)
    for axis, o in hops:
        message(KV_HEADS, axis, o, send_x, arr_x).start()

    seg_row = seg_ref[...]
    seg_col = column(seg_row)
    allowed = (seg_col == seg_row) & (iota((rows, rows), 0) <= iota((rows, rows), 1))
    bias[...] = jnp.where(allowed, 0.0, -1e30)
    first = jnp.sum(jnp.where(seg_row < seg_col, 1.0, 0.0), axis=1, keepdims=True)
    position = iota((rows, HEAD), 0).astype(F32) - first
    lane = iota((rows, HEAD), 1)
    half = lane % (HEAD // 2)
    frequency = jnp.exp(half.astype(F32) * (-2.0 * math.log(ROPE_THETA) / HEAD))
    angles = position * frequency
    cos_v[...] = jnp.cos(angles)
    sin_v[...] = jnp.where(lane < HEAD // 2, jnp.sin(angles), -jnp.sin(angles))
    lift[...] = jnp.zeros_like(lift)

    scale = 1.0 / math.sqrt(HEAD)
    exp_scale = scale * math.log2(math.e)
    up_row = iota((2 * ADAPTER_RANK, HEAD), 0)

    def cot_copies(j):
        return (
            pltpu.make_async_copy(
                keys_out.at[j],
                cot_hbm.at[:, pl.ds(pl.multiple_of(j * HEAD, HEAD), HEAD)],
                out_sem.at[j, 0],
            ),
            pltpu.make_async_copy(
                vals_out.at[j],
                cot_hbm.at[:, pl.ds(pl.multiple_of(KEY_HEAD_WIDTH + j * HEAD, HEAD), HEAD)],
                out_sem.at[j, 1],
            ),
        )

    def head(j, carry):
        for axis, o in hops:
            arrival(j, axis, o, send.at[j], arr.at[j]).wait_recv()
        arrived = arr[j].reshape(entries, GQ)
        for c in range(4):
            part = dot(own_hot[...], stage[j, :, c * GQ : (c + 1) * GQ])
            part += dot(arr_hot[c], arrived)
            pk[:, c * GQ : (c + 1) * GQ] = part.astype(BF16)
        k = pk[:, 2 * GROUP * HEAD : (2 * GROUP + 1) * HEAD]
        v = pk[:, (2 * GROUP + 1) * HEAD :]
        d_key = jnp.zeros((rows, HEAD), F32)
        d_val = jnp.zeros((rows, HEAD), F32)
        for h in range(GROUP):
            q = pk[:, h * HEAD : (h + 1) * HEAD]
            g = pk[:, (GROUP + h) * HEAD : (GROUP + h + 1) * HEAD]
            scores = dot_t(k, q) + bias[...]
            top = jnp.max(scores, axis=0, keepdims=True)
            weights = jnp.exp2((scores - top) * exp_scale)
            probs = weights * (1.0 / jnp.sum(weights, axis=0, keepdims=True))
            prob_grad = dot_t(v, g)
            delta = jnp.sum(probs * prob_grad, axis=0, keepdims=True)
            score_grad = (probs * (prob_grad - delta)).astype(BF16)
            d_val += dot(probs.astype(BF16), g)
            d_key += dot(score_grad, q)
        d_key = d_key * scale
        d_key = d_key * cos_v[...] + pltpu.roll(d_key, HEAD // 2, 1) * sin_v[...]
        key_low = d_key.astype(BF16)
        val_low = d_val.astype(BF16)
        keys_out[j] = key_low
        vals_out[j] = val_low
        for copy in cot_copies(j):
            copy.start()
        up = up_ref[:, pl.ds(pl.multiple_of(j * HEAD, HEAD), HEAD)].astype(F32)
        up_key = jnp.where(up_row < ADAPTER_RANK, up, 0.0).astype(BF16)
        up_val = jnp.where(up_row < ADAPTER_RANK, 0.0, up).astype(BF16)
        lift[...] += dot_t(key_low, up_key) + dot_t(val_low, up_val)
        return carry

    lax.fori_loop(0, KV_HEADS, head, 0)

    for axis, o in hops:
        arrival(KV_HEADS, axis, o, send_x, arr_x).wait_recv()
    arrived = arr_x[...].reshape(entries, xq)
    down_copy.wait()
    down_out = jnp.zeros((rows, 2 * ADAPTER_RANK), F32)
    lift_low = lift[...].astype(BF16)
    for c in range(4):
        part = dot(own_hot[...], x_st[:, c * xq : (c + 1) * xq])
        part += dot(arr_hot[c], arrived)
        part = part.astype(BF16)
        xp[...] = part
        down_out += dot(part, down_v[c * xq : (c + 1) * xq, :])
        ddown_ref[c * xq : (c + 1) * xq, :] = dot_l(xp[...], lift_low)
    down_low = down_out.astype(BF16)
    down_lane = iota((HEAD, 2 * ADAPTER_RANK), 1) < ADAPTER_RANK

    def up_grad(j, carry):
        from_key = dot_l(keys_out[j], down_low)
        from_val = dot_l(vals_out[j], down_low)
        dup_ref[pl.ds(pl.multiple_of(j * HEAD, HEAD), HEAD), :] = jnp.where(
            down_lane, from_key, from_val
        )
        return carry

    lax.fori_loop(0, KV_HEADS, up_grad, 0)

    def finish(j, carry):
        for copy in cot_copies(j):
            copy.wait()
        for axis, o in hops:
            message(j, axis, o, send.at[j], arr.at[j]).wait_send()
        return carry

    lax.fori_loop(0, KV_HEADS, finish, 0)
    for axis, o in hops:
        message(KV_HEADS, axis, o, send_x, arr_x).wait_send()


def sum_kernel(
    n_local,
    n_node,
    factor,
    a_ref,
    b_ref,
    a_out,
    b_out,
    send_a,
    recv_a,
    send_b,
    recv_b,
    send_c,
    recv_c,
    mid,
    last,
    sem_a,
    sem_b,
    sem_c,
):
    n_x, n_z = n_local // 2, n_node // 2
    own_l = lax.axis_index("local")
    own_n = lax.axis_index("node")
    core, lx = lax.rem(own_l, 2), own_l // 2
    y, z = lax.rem(own_n, 2), own_n // 2
    a_rows = a_ref.shape[4]
    n_group = 2 * n_x
    own_g = y * n_x + lx
    mesh_id = pl.DeviceIdType.MESH

    sibling = {"local": lx * 2 + (1 - core), "node": own_n}
    group = []
    for o in range(1, n_group):
        g = lax.rem(own_g + o, n_group)
        group.append((g, {"local": lax.rem(g, n_x) * 2 + core, "node": z * 2 + g // n_x}))
    far = []
    for o in range(1, n_z):
        t = lax.rem(z + o, n_z)
        far.append((t, {"local": own_l, "node": t * 2 + y}))

    barrier = pltpu.get_barrier_semaphore()
    targets = [sibling] + [d for _, d in group] + [d for _, d in far]
    for d in targets:
        pl.semaphore_signal(barrier, inc=1, device_id=d, device_id_type=mesh_id)

    for yy in range(2):
        for xx in range(n_x):
            g = yy * n_x + xx
            send_a[g, :, :a_rows, :] = a_ref[:, yy, xx, 1 - core].astype(BF16)
            send_a[g, :, a_rows:, :] = b_ref[:, yy, xx, 1 - core].astype(BF16)
    pl.semaphore_wait(barrier, len(targets))
    copies_a = []
    for o in range(n_group):
        g = lax.rem(own_g + 1 + o, n_group)
        copy = pltpu.make_async_remote_copy(
            src_ref=send_a.at[g],
            dst_ref=recv_a.at[g],
            send_sem=sem_a.at[0, g],
            recv_sem=sem_a.at[1, g],
            device_id=sibling,
            device_id_type=mesh_id,
        )
        copy.start()
        copies_a.append((g, copy))

    copies_b = []
    for o in range(n_group):
        g, copy = copies_a[o]
        copy.wait_recv()
        yy, xx = g // n_x, lax.rem(g, n_x)
        top = a_ref[:, yy, xx, core] + recv_a[g, :, :a_rows, :].astype(F32)
        low = b_ref[:, yy, xx, core] + recv_a[g, :, a_rows:, :].astype(F32)
        if o < n_group - 1:
            send_b[g, :, :a_rows, :] = top.astype(BF16)
            send_b[g, :, a_rows:, :] = low.astype(BF16)
            out = pltpu.make_async_remote_copy(
                src_ref=send_b.at[g],
                dst_ref=recv_b.at[own_g],
                send_sem=sem_b.at[0, g],
                recv_sem=sem_b.at[1, own_g],
                device_id=group[o][1],
                device_id_type=mesh_id,
            )
            out.start()
            copies_b.append(out)
        else:
            mid[:, :a_rows, :] = top
            mid[:, a_rows:, :] = low

    for g, d in group:
        pltpu.make_async_remote_copy(
            src_ref=send_b.at[g],
            dst_ref=recv_b.at[g],
            send_sem=sem_b.at[0, g],
            recv_sem=sem_b.at[1, g],
            device_id=d,
            device_id_type=mesh_id,
        ).wait_recv()
        mid[...] += recv_b[g].astype(F32)

    copies_c = []
    for t, d in far:
        send_c[t] = mid[t].astype(BF16)
        out = pltpu.make_async_remote_copy(
            src_ref=send_c.at[t],
            dst_ref=recv_c.at[z],
            send_sem=sem_c.at[0, t],
            recv_sem=sem_c.at[1, z],
            device_id=d,
            device_id_type=mesh_id,
        )
        out.start()
        copies_c.append(out)
    last[...] = mid[z]
    for t, d in far:
        pltpu.make_async_remote_copy(
            src_ref=send_c.at[t],
            dst_ref=recv_c.at[t],
            send_sem=sem_c.at[0, t],
            recv_sem=sem_c.at[1, t],
            device_id=d,
            device_id_type=mesh_id,
        ).wait_recv()
        last[...] += recv_c[t].astype(F32)
    a_out[...] = last[:a_rows, :] * factor
    b_out[...] = last[a_rows:, :] * factor
    for _, copy in copies_a:
        copy.wait_send()
    for copy in copies_b + copies_c:
        copy.wait_send()


def factor_sums(n_local, n_node, factor, a, b):
    n_x, n_z = n_local // 2, n_node // 2
    n_dev = n_local * n_node

    def lay(v):
        size = v.shape[0] // n_dev
        padded = -(-size // 16) * 16
        v = v.reshape(n_dev, size, v.shape[1])
        if padded != size:
            v = jnp.pad(v, ((0, 0), (0, padded - size), (0, 0)))
        return v.reshape(n_z, 2, n_x, 2, padded, v.shape[2]), size, padded

    a, a_size, a_rows = lay(a)
    b, b_size, b_rows = lay(b)
    rows = a_rows + b_rows
    wide = a.shape[-1]
    n_group = 2 * n_x
    vmem = pl.BlockSpec(memory_space=pltpu.VMEM)
    a_out, b_out = pl.pallas_call(
        functools.partial(sum_kernel, n_local, n_node, factor),
        out_shape=(
            jax.ShapeDtypeStruct((a_rows, wide), F32),
            jax.ShapeDtypeStruct((b_rows, wide), F32),
        ),
        in_specs=[vmem, vmem],
        out_specs=(vmem, vmem),
        scratch_shapes=[
            pltpu.VMEM((n_group, n_z, rows, wide), BF16),
            pltpu.VMEM((n_group, n_z, rows, wide), BF16),
            pltpu.VMEM((n_group, n_z, rows, wide), BF16),
            pltpu.VMEM((n_group, n_z, rows, wide), BF16),
            pltpu.VMEM((n_z, rows, wide), BF16),
            pltpu.VMEM((n_z, rows, wide), BF16),
            pltpu.VMEM((n_z, rows, wide), F32),
            pltpu.VMEM((rows, wide), F32),
            pltpu.SemaphoreType.DMA((2, n_group)),
            pltpu.SemaphoreType.DMA((2, n_group)),
            pltpu.SemaphoreType.DMA((2, n_z)),
        ],
        compiler_params=pltpu.CompilerParams(
            collective_id=1, has_side_effects=True, vmem_limit_bytes=48 * 2**20
        ),
        name="factor_sums",
    )(a, b)
    return a_out[:a_size], b_out[:b_size]


def local(n_local, n_node, *args):
    activations, queries, rotated_key_value, attention_out_grad, adapter_down, adapter_up = args[:6]
    rows, width = activations.shape
    peers = n_local + n_node
    entries = peers * CHUNK
    vmem = pl.BlockSpec(memory_space=pltpu.VMEM)
    hbm = pl.BlockSpec(memory_space=pl.ANY)
    cotangent, down_grad, up_grad = pl.pallas_call(
        functools.partial(main_kernel, n_local, n_node),
        out_shape=(
            jax.ShapeDtypeStruct((rows, 2 * KEY_HEAD_WIDTH), BF16),
            jax.ShapeDtypeStruct((width, 2 * ADAPTER_RANK), F32),
            jax.ShapeDtypeStruct((KEY_HEAD_WIDTH, 2 * ADAPTER_RANK), F32),
        ),
        in_specs=[hbm] * 5 + [vmem] * 7,
        out_specs=(hbm, vmem, vmem),
        scratch_shapes=[
            pltpu.VMEM((KV_HEADS, rows, GW), BF16),
            pltpu.VMEM((rows, width), BF16),
            pltpu.VMEM((width, 2 * ADAPTER_RANK), BF16),
            pltpu.VMEM((KV_HEADS, peers, CHUNK, GQ), BF16),
            pltpu.VMEM((peers, CHUNK, width // 4), BF16),
            pltpu.VMEM((KV_HEADS, peers, CHUNK, GQ), BF16),
            pltpu.VMEM((peers, CHUNK, width // 4), BF16),
            pltpu.VMEM((4, entries, rows), BF16),
            pltpu.VMEM((rows, rows), BF16),
            pltpu.VMEM((4, rows, entries), BF16),
            pltpu.VMEM((rows, rows), F32),
            pltpu.VMEM((rows, HEAD), F32),
            pltpu.VMEM((rows, HEAD), F32),
            pltpu.VMEM((rows, GW), BF16),
            pltpu.VMEM((rows, width // 4), BF16),
            pltpu.VMEM((KV_HEADS, rows, HEAD), BF16),
            pltpu.VMEM((KV_HEADS, rows, HEAD), BF16),
            pltpu.VMEM((rows, 2 * ADAPTER_RANK), F32),
            pltpu.SemaphoreType.DMA((KV_HEADS, 4)),
            pltpu.SemaphoreType.DMA((2,)),
            pltpu.SemaphoreType.DMA((KV_HEADS, 2)),
            pltpu.SemaphoreType.DMA((KV_HEADS + 1, peers)),
            pltpu.SemaphoreType.DMA((KV_HEADS + 1, peers)),
        ],
        compiler_params=pltpu.CompilerParams(
            collective_id=0, has_side_effects=True, vmem_limit_bytes=48 * 2**20
        ),
        name="exchange_attention",
    )(*args)
    factor = 1.0 / math.sqrt(rows * n_local * n_node)
    down_sum, up_sum = factor_sums(n_local, n_node, factor, down_grad, up_grad)
    return cotangent, down_sum, up_sum


def solution(mesh):
    placed = (P(("node", "local"), None),) * 4 + (P(),) * 2 + (P(("node", "local"), None),) * 6
    return jax.shard_map(
        functools.partial(local, mesh.shape["local"], mesh.shape["node"]),
        mesh=mesh,
        in_specs=placed,
        out_specs=(P(("node", "local"), None),) * 3,
        check_vma=False,
    )
```

time: 541 us -> 78.3 us (0.14); the launches traced: 531 us -> 77.9 us
  waiting for transfers between devices: 275 us -> 0 us
  local copies, waits for them, and re-layouts: 97.5 us -> 11.5 us
  matrix products: 66 us -> 0 us
  Pallas kernels: 0 us -> 65.8 us
  starting transfers between devices: 34.4 us -> 0 us
  other arithmetic: 27.4 us -> 0 us
  loops' own time: 15.9 us -> 0 us
  between operations: 14.8 us -> 0.68 us
    reduce_scatter x1 -> x0, waiting for transfers between devices: 135 us -> none  [local(): lax.psum_scatter(down_factor_grad, ('node', 'local'), scatter_dimension=0...]
    unnamed x3 -> x0, waiting for transfers between devices: 127 us -> none
    pallas_call x0 -> x2, Pallas kernels: none -> 65.8 us  [the longest x1 45.1 us: local(): pl.pallas_call(functools.partial(main_kernel, n_local, n_node), out_shape...]
    dot_general x30 -> x0, matrix products: 41.4 us -> none  [the longest x8 19.1 us: per_group(): jnp.einsum('sij,isd->jd', probs.astype(jnp.bfloat16), grad_block, preferr...]
    scatter x8 -> x0, local copies, waits for them, and re-layouts: 36 us -> none  [pack_rows(): return empty_rows.at[slot_ids].set(source_rows, mode='drop')]
    all_to_all x8 -> x0, starting transfers between devices: 34.2 us -> none  [the longest x1 6.38 us: local(): lax.all_to_all(pack_rows(rotated_key_value, node_slots, far_total), 'node...]
    gather x4 -> x0, local copies, waits for them, and re-layouts: 27.8 us -> none  [assemble(): return jnp.take(arrivals, arrival_pick_index, axis=0)]
    sub x8 -> x0, matrix products: 24.5 us -> none  [per_group(): weights = jnp.exp(scores - row_max)]
  transfers between devices with their start and end apart: 10 -> 0, of which waited for: 5 -> 0; matrix products, arithmetic and copies ran while one was open for 30% -> 0% of each run, Pallas kernels for 0% -> 0%
where the time goes in v1:
time: 78.3 us; the launch traced here: 77.9 us
  Pallas kernels  65.8 us (84%)
  local copies, waits for them, and re-layouts  11.5 us (15%)
    pallas_call x1, Pallas kernels, local(): pl.pallas_call(functools.partial(main_kernel, n_local, n_node), out_shape...  45.1 us
    pallas_call x1, Pallas kernels, factor_sums(): pl.pallas_call(functools.partial(sum_kernel, n_local, n_node, factor), ou...  20.6 us
    unnamed x23, local copies, waits for them, and re-layouts  11.5 us

profile of v1, /device:TPU:0, one launch (start us, length us, event | category | flops | bytes accessed | tf_op | source)
XLA Modules:
  0.0 77.9 jit_solution(4372763513800866565)
XLA Ops:
  0.6 0.0 copy-start.1
  0.6 1.3 %copy-done.1 = bf16[5120,128]{1,0:T(8,128)(2,1)S(1)} copy-done((bf16[5120,128]{1,0:T(8,128)(2,1)S(1)}, bf16[5120,128]{1,0:T(8,128)(2,1)}, u32[]{:S(2)}) %copy-start.1) | copy-done | bytes 1310744
  2.0 0.0 copy-start.2
  2.0 1.2 %copy-done.2 = bf16[256,2048]{1,0:T(8,128)(2,1)S(1)} copy-done((bf16[256,2048]{1,0:T(8,128)(2,1)S(1)}, bf16[256,2048]{1,0:T(8,128)(2,1)}, u32[]{:S(2)}) %copy-start.2) | copy-done | bytes 1048600
  3.2 0.0 copy-start.3
  3.2 0.9 %copy-done.3 = bf16[128,1024]{1,0:T(8,128)(2,1)S(1)} copy-done((bf16[128,1024]{1,0:T(8,128)(2,1)S(1)}, bf16[128,1024]{1,0:T(8,128)(2,1)}, u32[]{:S(2)}) %copy-start.3) | copy-done | bytes 262168
  4.1 0.0 copy-start.4
  4.1 0.7 copy-done.4
  4.8 0.0 copy-start.5
  4.8 0.7 copy-done.5
  5.5 0.0 copy-start.6
  5.5 0.7 copy-done.6
  6.2 0.0 copy-start.7
  6.2 0.7 copy-done.7
  6.8 0.0 copy-start.8
  6.8 0.7 copy-done.8
  7.5 0.0 copy-start.9
  7.5 0.7 copy-done.9
  8.2 45.1 %exchange_attention.1 = (bf16[256,2048]{1,0:T(8,128)(2,1)S(1)}, f32[5120,128]{1,0:T(8,128)}, f32[1024,128]{1,0:T(8,128)S(1)}) custom-call(bf16[256,5120]{1,0:T(8,128)(2,1)} %x_hbm.1, bf16[256,5120]{1,0:T(8,128)(2,1)} %q_hbm.1, bf16[256,2048]{1,0:T(8,128)(2,1)S(1)} %copy-done.2, bf16[256,5120]{1,0:T(8,128)(2,1)} %g_hbm.1, bf16[5120,128]{1,0:T(8,128)(2,1)S(1)} %copy-done.1, ...), custom_call_target="tpu_custom_call" | custom-call | tf_op jit(solution)/shard_map/exchange_attention/pallas_call | solution.py:516
  53.3 0.0 copy-start
  53.3 1.7 %copy-done = f32[5120,128]{1,0:T(8,128)S(1)} copy-done((f32[5120,128]{1,0:T(8,128)S(1)}, f32[5120,128]{1,0:T(8,128)}, u32[]{:S(2)}) %copy-start) | copy-done | bytes 2621464
  55.1 20.6 %factor_sums.1 = (f32[160,128]{1,0:T(8,128)S(1)}, f32[32,128]{1,0:T(8,128)S(1)}) custom-call(f32[4,2,2,2,160,128]{5,4,3,2,1,0:T(8,128)S(1)} %bitcast.2, f32[4,2,2,2,32,128]{5,4,3,2,1,0:T(8,128)S(1)} %bitcast.3), custom_call_target="tpu_custom_call" | custom-call | tf_op jit(solution)/shard_map/factor_sums/pallas_call | solution.py:480
  75.7 1.0 %copy.18 = bf16[256,2048]{1,0:T(8,128)(2,1)} copy(bf16[256,2048]{1,0:T(8,128)(2,1)S(1)} %get-tuple-element.16) | data formatting | bytes 2097152
  76.7 0.6 copy.19
  77.3 0.6 copy.20
Async XLA Ops:
  0.6 1.3 %copy-start.1 = (bf16[5120,128]{1,0:T(8,128)(2,1)S(1)}, bf16[5120,128]{1,0:T(8,128)(2,1)}, u32[]{:S(2)}) copy-start(bf16[5120,128]{1,0:T(8,128)(2,1)} %down_hbm.1) | copy-start | bytes 3932164
  2.0 1.2 %copy-start.2 = (bf16[256,2048]{1,0:T(8,128)(2,1)S(1)}, bf16[256,2048]{1,0:T(8,128)(2,1)}, u32[]{:S(2)}) copy-start(bf16[256,2048]{1,0:T(8,128)(2,1)} %kv_hbm.1) | copy-start | bytes 3145732
  3.2 0.9 %copy-start.3 = (bf16[128,1024]{1,0:T(8,128)(2,1)S(1)}, bf16[128,1024]{1,0:T(8,128)(2,1)}, u32[]{:S(2)}) copy-start(bf16[128,1024]{1,0:T(8,128)(2,1)} %up_ref.1) | copy-start | bytes 786436
  4.1 0.7 copy-start.4
  4.8 0.7 copy-start.5
  5.5 0.7 copy-start.6
  6.2 0.7 copy-start.7
  6.8 0.7 copy-start.8
  7.5 0.7 copy-start.9
  53.3 1.7 %copy-start = (f32[5120,128]{1,0:T(8,128)S(1)}, f32[5120,128]{1,0:T(8,128)}, u32[]{:S(2)}) copy-start(f32[5120,128]{1,0:T(8,128)} %get-tuple-element.9) | copy-start | bytes 7864324

commit v2 on v1

--- a/solution.py
+++ b/solution.py
@@ -53,34 +53,44 @@
     kv_hbm,
     g_hbm,
     down_hbm,
-    up_ref,
-    bl_ref,
-    bo_ref,
-    sn_ref,
-    so_ref,
-    pick_ref,
-    seg_ref,
+    up_hbm,
+    bl_hbm,
+    bo_hbm,
+    sn_hbm,
+    so_hbm,
+    pick_hbm,
+    seg_hbm,
     cot_hbm,
     ddown_ref,
     dup_ref,
+    ints,
+    up_ref,
     stage,
     x_st,
+    x_turned,
     down_v,
+    down_rows,
     send,
-    send_x,
+    send_d,
+    send_l,
     arr,
-    arr_x,
+    arr_d,
+    arr_l,
     pack_hot,
     own_hot,
     arr_hot,
     bias,
     cos_v,
     sin_v,
-    pk,
-    xp,
+    qs,
+    gs,
+    kvs,
+    probs_s,
+    grads_s,
     keys_out,
     vals_out,
     lift,
+    int_sem,
     load_sem,
     xload_sem,
     out_sem,
@@ -89,7 +99,7 @@
 ):
     rows = x_st.shape[0]
     width = x_st.shape[1]
-    xq = width // 4
+    block = HEAD
     own_l = lax.axis_index("local")
     own_n = lax.axis_index("node")
     peers = n_local + n_node
@@ -115,6 +125,13 @@
 
     x_copy = pltpu.make_async_copy(x_hbm, x_st, xload_sem.at[0])
     down_copy = pltpu.make_async_copy(down_hbm, down_v, xload_sem.at[1])
+    up_copy = pltpu.make_async_copy(up_hbm, up_ref, xload_sem.at[2])
+    int_copies = [
+        pltpu.make_async_copy(src, ints.at[i], int_sem.at[i])
+        for i, src in enumerate((bl_hbm, bo_hbm, sn_hbm, so_hbm, pick_hbm, seg_hbm))
+    ]
+    for copy in int_copies:
+        copy.start()
 
     barrier = pltpu.get_barrier_semaphore()
     for o in range(1, n_local):
@@ -140,19 +157,23 @@
     lax.fori_loop(0, KV_HEADS, start_load, 0)
     x_copy.start()
     down_copy.start()
-
-    moved_in = bl_ref[...] != own_l
-    moved_out = sn_ref[...] != own_n
+    up_copy.start()
+    for copy in int_copies:
+        copy.wait()
+    near_bin, near_off, far_bin, far_off = ints[0], ints[1], ints[2], ints[3]
+
+    moved_in = near_bin != own_l
+    moved_out = far_bin != own_n
     code = jnp.where(
         moved_in,
-        bl_ref[...] * CAP + bo_ref[...],
-        jnp.where(moved_out, (n_local + sn_ref[...]) * CAP + so_ref[...], -1),
+        near_bin * CAP + near_off,
+        jnp.where(moved_out, (n_local + far_bin) * CAP + far_off, -1),
     )
     a_sub = iota((entries, rows), 0)
     hit = code == (a_sub // CHUNK) * CAP + a_sub % CAP
     for c in range(4):
         pack_hot[c] = jnp.where(hit & ((a_sub // CAP) % 4 == c), 1.0, 0.0).astype(BF16)
-    pick = column(pick_ref[...])
+    pick = column(ints[4])
     own_hot[...] = jnp.where(pick == iota((rows, rows), 1), 1.0, 0.0).astype(BF16)
     a_lane = iota((rows, entries), 1)
     got = pick == rows + (a_lane // CHUNK) * CAP + a_lane % CAP
@@ -160,7 +181,8 @@
         arr_hot[c] = jnp.where(got & ((a_lane // CAP) % 4 == c), 1.0, 0.0).astype(BF16)
 
     for slot in (own_l, n_local + own_n):
-        arr_x[slot] = jnp.zeros(arr_x.shape[1:], BF16)
+        arr_d[slot] = jnp.zeros(arr_d.shape[1:], BF16)
+        arr_l[slot] = jnp.zeros(arr_l.shape[1:], BF16)
 
     def clear(j, c):
         for slot in (own_l, n_local + own_n):
@@ -210,14 +232,13 @@
 
     lax.fori_loop(0, KV_HEADS, pack, 0)
     x_copy.wait()
-    total = dot(pack_hot[0], x_st[:, 0:xq])
-    for c in range(1, 4):
-        total += dot(pack_hot[c], x_st[:, c * xq : (c + 1) * xq])
-    send_x[...] = total.astype(BF16).reshape(peers, CHUNK, xq)
+    down_copy.wait()
+    down_rows[...] = dot(x_st[...], down_v[...]).astype(BF16)
+    send_d[...] = dot(pack_hot[0], down_rows[...]).astype(BF16).reshape(send_d.shape)
     for axis, o in hops:
-        message(KV_HEADS, axis, o, send_x, arr_x).start()
-
-    seg_row = seg_ref[...]
+        message(KV_HEADS, axis, o, send_d, arr_d).start()
+
+    seg_row = ints[5]
     seg_col = column(seg_row)
     allowed = (seg_col == seg_row) & (iota((rows, rows), 0) <= iota((rows, rows), 1))
     bias[...] = jnp.where(allowed, 0.0, -1e30)
@@ -231,6 +252,14 @@
     sin_v[...] = jnp.where(lane < HEAD // 2, jnp.sin(angles), -jnp.sin(angles))
     lift[...] = jnp.zeros_like(lift)
 
+    def turn(i, carry):
+        at = pl.multiple_of(i * HEAD, HEAD)
+        x_turned[pl.ds(at, HEAD), :] = jnp.transpose(x_st[:, pl.ds(at, HEAD)])
+        return carry
+
+    lax.fori_loop(0, width // HEAD, turn, 0)
+    up_copy.wait()
+
     scale = 1.0 / math.sqrt(HEAD)
     exp_scale = scale * math.log2(math.e)
     up_row = iota((2 * ADAPTER_RANK, HEAD), 0)
@@ -256,23 +285,40 @@
         for c in range(4):
             part = dot(own_hot[...], stage[j, :, c * GQ : (c + 1) * GQ])
             part += dot(arr_hot[c], arrived)
-            pk[:, c * GQ : (c + 1) * GQ] = part.astype(BF16)
-        k = pk[:, 2 * GROUP * HEAD : (2 * GROUP + 1) * HEAD]
-        v = pk[:, (2 * GROUP + 1) * HEAD :]
-        d_key = jnp.zeros((rows, HEAD), F32)
-        d_val = jnp.zeros((rows, HEAD), F32)
-        for h in range(GROUP):
-            q = pk[:, h * HEAD : (h + 1) * HEAD]
-            g = pk[:, (GROUP + h) * HEAD : (GROUP + h + 1) * HEAD]
-            scores = dot_t(k, q) + bias[...]
-            top = jnp.max(scores, axis=0, keepdims=True)
-            weights = jnp.exp2((scores - top) * exp_scale)
-            probs = weights * (1.0 / jnp.sum(weights, axis=0, keepdims=True))
-            prob_grad = dot_t(v, g)
-            delta = jnp.sum(probs * prob_grad, axis=0, keepdims=True)
-            score_grad = (probs * (prob_grad - delta)).astype(BF16)
-            d_val += dot(probs.astype(BF16), g)
-            d_key += dot(score_grad, q)
+            part = part.astype(BF16)
+            for i in range(3):
+                col = c * 3 + i
+                piece = part[:, i * HEAD : (i + 1) * HEAD]
+                if col >= 2 * GROUP:
+                    kvs[col - 2 * GROUP] = piece
+                    continue
+                dst, h = (qs, col) if col < GROUP else (gs, col - GROUP)
+                for b in range(rows // block):
+                    dst[b, h * block : (h + 1) * block, :] = piece[b * block : (b + 1) * block]
+        d_keys = [jnp.zeros((block, HEAD), F32)] * (rows // block)
+        d_vals = [jnp.zeros((block, HEAD), F32)] * (rows // block)
+        for b in range(rows // block):
+            seen = (b + 1) * block
+            scores = dot_t(kvs[0, :seen, :], qs[b])
+            prob_grads = dot_t(kvs[1, :seen, :], gs[b])
+            mask = bias[:seen, b * block : (b + 1) * block]
+            for h in range(GROUP):
+                cols = slice(h * block, (h + 1) * block)
+                score = scores[:, cols] + mask
+                top = jnp.max(score, axis=0, keepdims=True)
+                weights = jnp.exp2((score - top) * exp_scale)
+                probs = weights * (1.0 / jnp.sum(weights, axis=0, keepdims=True))
+                prob_grad = prob_grads[:, cols]
+                delta = jnp.sum(probs * prob_grad, axis=0, keepdims=True)
+                probs_s[b, :seen, cols] = probs.astype(BF16)
+                grads_s[b, :seen, cols] = (probs * (prob_grad - delta)).astype(BF16)
+            d_val = dot(probs_s[b, :seen, :], gs[b])
+            d_key = dot(grads_s[b, :seen, :], qs[b])
+            for t in range(b + 1):
+                d_vals[t] += d_val[t * block : (t + 1) * block]
+                d_keys[t] += d_key[t * block : (t + 1) * block]
+        d_key = jnp.concatenate(d_keys, axis=0)
+        d_val = jnp.concatenate(d_vals, axis=0)
         d_key = d_key * scale
         d_key = d_key * cos_v[...] + pltpu.roll(d_key, HEAD // 2, 1) * sin_v[...]
         key_low = d_key.astype(BF16)
@@ -289,19 +335,15 @@
 
     lax.fori_loop(0, KV_HEADS, head, 0)
 
+    lift_low = lift[...].astype(BF16)
+    send_l[...] = dot_l(arr_hot[0], lift_low).astype(BF16).reshape(send_l.shape)
     for axis, o in hops:
-        arrival(KV_HEADS, axis, o, send_x, arr_x).wait_recv()
-    arrived = arr_x[...].reshape(entries, xq)
-    down_copy.wait()
-    down_out = jnp.zeros((rows, 2 * ADAPTER_RANK), F32)
-    lift_low = lift[...].astype(BF16)
-    for c in range(4):
-        part = dot(own_hot[...], x_st[:, c * xq : (c + 1) * xq])
-        part += dot(arr_hot[c], arrived)
-        part = part.astype(BF16)
-        xp[...] = part
-        down_out += dot(part, down_v[c * xq : (c + 1) * xq, :])
-        ddown_ref[c * xq : (c + 1) * xq, :] = dot_l(xp[...], lift_low)
+        message(KV_HEADS + 1, axis, o, send_l, arr_l).start()
+
+    for axis, o in hops:
+        arrival(KV_HEADS, axis, o, send_d, arr_d).wait_recv()
+    down_out = dot(own_hot[...], down_rows[...])
+    down_out += dot(arr_hot[0], arr_d[...].reshape(entries, HEAD))
     down_low = down_out.astype(BF16)
     down_lane = iota((HEAD, 2 * ADAPTER_RANK), 1) < ADAPTER_RANK
 
@@ -314,6 +356,17 @@
         return carry
 
     lax.fori_loop(0, KV_HEADS, up_grad, 0)
+
+    own_lift = dot_l(own_hot[...], lift_low)
+    for axis, o in hops:
+        arrival(KV_HEADS + 1, axis, o, send_l, arr_l).wait_recv()
+    own_lift += dot_l(pack_hot[0], arr_l[...].reshape(entries, HEAD))
+    own_lift = own_lift.astype(BF16)
+    span = width // 8
+    for c in range(8):
+        ddown_ref[c * span : (c + 1) * span, :] = dot(
+            x_turned[c * span : (c + 1) * span, :], own_lift
+        )
 
     def finish(j, carry):
         for copy in cot_copies(j):
@@ -324,7 +377,8 @@
 
     lax.fori_loop(0, KV_HEADS, finish, 0)
     for axis, o in hops:
-        message(KV_HEADS, axis, o, send_x, arr_x).wait_send()
+        message(KV_HEADS, axis, o, send_d, arr_d).wait_send()
+        message(KV_HEADS + 1, axis, o, send_l, arr_l).wait_send()
 
 
 def sum_kernel(
@@ -520,32 +574,42 @@
             jax.ShapeDtypeStruct((width, 2 * ADAPTER_RANK), F32),
             jax.ShapeDtypeStruct((KEY_HEAD_WIDTH, 2 * ADAPTER_RANK), F32),
         ),
-        in_specs=[hbm] * 5 + [vmem] * 7,
+        in_specs=[hbm] * 12,
         out_specs=(hbm, vmem, vmem),
         scratch_shapes=[
+            pltpu.VMEM((6, 1, rows), jnp.int32),
+            pltpu.VMEM(adapter_up.shape, BF16),
             pltpu.VMEM((KV_HEADS, rows, GW), BF16),
             pltpu.VMEM((rows, width), BF16),
+            pltpu.VMEM((width, rows), BF16),
             pltpu.VMEM((width, 2 * ADAPTER_RANK), BF16),
+            pltpu.VMEM((rows, 2 * ADAPTER_RANK), BF16),
             pltpu.VMEM((KV_HEADS, peers, CHUNK, GQ), BF16),
-            pltpu.VMEM((peers, CHUNK, width // 4), BF16),
+            pltpu.VMEM((peers, CHUNK, 2 * ADAPTER_RANK), BF16),
+            pltpu.VMEM((peers, CHUNK, 2 * ADAPTER_RANK), BF16),
             pltpu.VMEM((KV_HEADS, peers, CHUNK, GQ), BF16),
-            pltpu.VMEM((peers, CHUNK, width // 4), BF16),
+            pltpu.VMEM((peers, CHUNK, 2 * ADAPTER_RANK), BF16),
+            pltpu.VMEM((peers, CHUNK, 2 * ADAPTER_RANK), BF16),
             pltpu.VMEM((4, entries, rows), BF16),
             pltpu.VMEM((rows, rows), BF16),
             pltpu.VMEM((4, rows, entries), BF16),
             pltpu.VMEM((rows, rows), F32),
             pltpu.VMEM((rows, HEAD), F32),
             pltpu.VMEM((rows, HEAD), F32),
-            pltpu.VMEM((rows, GW), BF16),
-            pltpu.VMEM((rows, width // 4), BF16),
+            pltpu.VMEM((rows // HEAD, GROUP * HEAD, HEAD), BF16),
+            pltpu.VMEM((rows // HEAD, GROUP * HEAD, HEAD), BF16),
+            pltpu.VMEM((2, rows, HEAD), BF16),
+            pltpu.VMEM((rows // HEAD, rows, GROUP * HEAD), BF16),
+            pltpu.VMEM((rows // HEAD, rows, GROUP * HEAD), BF16),
             pltpu.VMEM((KV_HEADS, rows, HEAD), BF16),
             pltpu.VMEM((KV_HEADS, rows, HEAD), BF16),
             pltpu.VMEM((rows, 2 * ADAPTER_RANK), F32),
+            pltpu.SemaphoreType.DMA((6,)),
             pltpu.SemaphoreType.DMA((KV_HEADS, 4)),
-            pltpu.SemaphoreType.DMA((2,)),
+            pltpu.SemaphoreType.DMA((3,)),
             pltpu.SemaphoreType.DMA((KV_HEADS, 2)),
-            pltpu.SemaphoreType.DMA((KV_HEADS + 1, peers)),
-            pltpu.SemaphoreType.DMA((KV_HEADS + 1, peers)),
+            pltpu.SemaphoreType.DMA((KV_HEADS + 2, peers)),
+            pltpu.SemaphoreType.DMA((KV_HEADS + 2, peers)),
         ],
         compiler_params=pltpu.CompilerParams(
             collective_id=0, has_side_effects=True, vmem_limit_bytes=48 * 2**20

time: 78.3 us -> 73.6 us (0.940)
  Pallas kernels: 65.8 us -> 61.1 us
    pallas_call x1, Pallas kernels: 45.1 us -> 42.3 us  [local(): pl.pallas_call(functools.partial(main_kernel, n_local, n_node), out_shape...]
    pallas_call x1, Pallas kernels: 20.6 us -> 18.8 us  [factor_sums(): pl.pallas_call(functools.partial(sum_kernel, n_local, n_node, factor), ou...]
where the time goes in v2:
time: 73.6 us; the launch traced here: 73.3 us
  Pallas kernels  61.1 us (83%)
  local copies, waits for them, and re-layouts  11.5 us (16%)
    pallas_call x1, Pallas kernels, local(): pl.pallas_call(functools.partial(main_kernel, n_local, n_node), out_shape...  42.3 us
    pallas_call x1, Pallas kernels, factor_sums(): pl.pallas_call(functools.partial(sum_kernel, n_local, n_node, factor), ou...  18.8 us
    unnamed x23, local copies, waits for them, and re-layouts  11.5 us

profile of v2, /device:TPU:0, one launch (start us, length us, event | category | flops | bytes accessed | tf_op | source)
XLA Modules:
  0.0 73.3 jit_solution(5800362317622538262)
XLA Ops:
  0.6 0.0 copy-start.1
  0.6 1.3 %copy-done.1 = bf16[5120,128]{1,0:T(8,128)(2,1)S(1)} copy-done((bf16[5120,128]{1,0:T(8,128)(2,1)S(1)}, bf16[5120,128]{1,0:T(8,128)(2,1)}, u32[]{:S(2)}) %copy-start.1) | copy-done | bytes 1310744
  2.0 0.0 copy-start.2
  2.0 1.2 %copy-done.2 = bf16[256,2048]{1,0:T(8,128)(2,1)S(1)} copy-done((bf16[256,2048]{1,0:T(8,128)(2,1)S(1)}, bf16[256,2048]{1,0:T(8,128)(2,1)}, u32[]{:S(2)}) %copy-start.2) | copy-done | bytes 1048600
  3.2 0.0 copy-start.3
  3.2 0.9 %copy-done.3 = bf16[128,1024]{1,0:T(8,128)(2,1)S(1)} copy-done((bf16[128,1024]{1,0:T(8,128)(2,1)S(1)}, bf16[128,1024]{1,0:T(8,128)(2,1)}, u32[]{:S(2)}) %copy-start.3) | copy-done | bytes 262168
  4.1 0.0 copy-start.4
  4.1 0.7 copy-done.4
  4.8 0.0 copy-start.5
  4.8 0.7 copy-done.5
  5.5 0.0 copy-start.6
  5.5 0.7 copy-done.6
  6.2 0.0 copy-start.7
  6.2 0.7 copy-done.7
  6.8 0.0 copy-start.8
  6.8 0.7 copy-done.8
  7.5 0.0 copy-start.9
  7.5 0.7 copy-done.9
  8.2 42.3 %exchange_attention.1 = (bf16[256,2048]{1,0:T(8,128)(2,1)S(1)}, f32[5120,128]{1,0:T(8,128)}, f32[1024,128]{1,0:T(8,128)S(1)}) custom-call(bf16[256,5120]{1,0:T(8,128)(2,1)} %x_hbm.1, bf16[256,5120]{1,0:T(8,128)(2,1)} %q_hbm.1, bf16[256,2048]{1,0:T(8,128)(2,1)S(1)} %copy-done.2, bf16[256,5120]{1,0:T(8,128)(2,1)} %g_hbm.1, bf16[5120,128]{1,0:T(8,128)(2,1)S(1)} %copy-done.1, ...), custom_call_target="tpu_custom_call" | custom-call | tf_op jit(solution)/shard_map/exchange_attention/pallas_call | solution.py:570
  50.5 0.0 copy-start
  50.5 1.7 %copy-done = f32[5120,128]{1,0:T(8,128)S(1)} copy-done((f32[5120,128]{1,0:T(8,128)S(1)}, f32[5120,128]{1,0:T(8,128)}, u32[]{:S(2)}) %copy-start) | copy-done | bytes 2621464
  52.2 18.8 %factor_sums.1 = (f32[160,128]{1,0:T(8,128)S(1)}, f32[32,128]{1,0:T(8,128)S(1)}) custom-call(f32[4,2,2,2,160,128]{5,4,3,2,1,0:T(8,128)S(1)} %bitcast.2, f32[4,2,2,2,32,128]{5,4,3,2,1,0:T(8,128)S(1)} %bitcast.3), custom_call_target="tpu_custom_call" | custom-call | tf_op jit(solution)/shard_map/factor_sums/pallas_call | solution.py:534
  71.1 1.0 %copy.18 = bf16[256,2048]{1,0:T(8,128)(2,1)} copy(bf16[256,2048]{1,0:T(8,128)(2,1)S(1)} %get-tuple-element.16) | data formatting | bytes 2097152
  72.0 0.6 copy.19
  72.7 0.6 copy.20
Async XLA Ops:
  0.6 1.3 %copy-start.1 = (bf16[5120,128]{1,0:T(8,128)(2,1)S(1)}, bf16[5120,128]{1,0:T(8,128)(2,1)}, u32[]{:S(2)}) copy-start(bf16[5120,128]{1,0:T(8,128)(2,1)} %down_hbm.1) | copy-start | bytes 3932164
  2.0 1.2 %copy-start.2 = (bf16[256,2048]{1,0:T(8,128)(2,1)S(1)}, bf16[256,2048]{1,0:T(8,128)(2,1)}, u32[]{:S(2)}) copy-start(bf16[256,2048]{1,0:T(8,128)(2,1)} %kv_hbm.1) | copy-start | bytes 3145732
  3.2 0.9 %copy-start.3 = (bf16[128,1024]{1,0:T(8,128)(2,1)S(1)}, bf16[128,1024]{1,0:T(8,128)(2,1)}, u32[]{:S(2)}) copy-start(bf16[128,1024]{1,0:T(8,128)(2,1)} %up_hbm.1) | copy-start | bytes 786436
  4.1 0.7 copy-start.4
  4.8 0.7 copy-start.5
  5.5 0.7 copy-start.6
  6.2 0.7 copy-start.7
  6.8 0.7 copy-start.8
  7.5 0.7 copy-start.9
  50.5 1.7 %copy-start = (f32[5120,128]{1,0:T(8,128)S(1)}, f32[5120,128]{1,0:T(8,128)}, u32[]{:S(2)}) copy-start(f32[5120,128]{1,0:T(8,128)} %get-tuple-element.9) | copy-start | bytes 7864324

commit v3 on v2

--- a/solution.py
+++ b/solution.py
@@ -17,7 +17,9 @@
 KEY_HEAD_WIDTH = 1024
 CHUNK = 16
 GW = (2 * GROUP + 2) * HEAD
-GQ = GW // 4
+PAIR = 2
+ROUNDS = KV_HEADS // PAIR
+GQ = PAIR * GW // 4
 ROPE_THETA = 1000000.0
 F32 = jnp.float32
 BF16 = jnp.bfloat16
@@ -48,6 +50,7 @@
 def main_kernel(
     n_local,
     n_node,
+    factor,
     x_hbm,
     q_hbm,
     kv_hbm,
@@ -61,42 +64,49 @@
     pick_hbm,
     seg_hbm,
     cot_hbm,
-    ddown_ref,
-    dup_ref,
-    ints,
-    up_ref,
-    stage,
-    x_st,
-    x_turned,
-    down_v,
-    down_rows,
-    send,
-    send_d,
-    send_l,
-    arr,
-    arr_d,
-    arr_l,
-    pack_hot,
-    own_hot,
-    arr_hot,
-    bias,
-    cos_v,
-    sin_v,
-    qs,
-    gs,
-    kvs,
-    probs_s,
-    grads_s,
-    keys_out,
-    vals_out,
-    lift,
-    int_sem,
-    load_sem,
-    xload_sem,
-    out_sem,
-    send_sem,
-    recv_sem,
+    *rest,
 ):
+    if factor is None:
+        ddown_ref, dup_ref = rest[:2]
+    else:
+        down_sum, up_sum = rest[:2]
+        dup_ref, send_a, recv_a, send_b, recv_b, send_c, recv_c = rest[-13:-6]
+        own_part, mid, last, sem_a, sem_b, sem_c = rest[-6:]
+    (
+        ints,
+        up_ref,
+        stage,
+        x_st,
+        x_turned,
+        down_v,
+        down_rows,
+        send,
+        send_d,
+        send_l,
+        arr,
+        arr_d,
+        arr_l,
+        pack_hot,
+        own_hot,
+        arr_hot,
+        bias,
+        cos_v,
+        sin_v,
+        qs,
+        gs,
+        kvs,
+        probs_s,
+        grads_s,
+        keys_out,
+        vals_out,
+        lift,
+        int_sem,
+        load_sem,
+        xload_sem,
+        out_sem,
+        send_sem,
+        recv_sem,
+    ) = rest[2:35]
     rows = x_st.shape[0]
     width = x_st.shape[1]
     block = HEAD
@@ -105,20 +115,23 @@
     peers = n_local + n_node
     entries = peers * CHUNK
 
-    def load(j):
+    def load(r):
         copies = []
-        spans = (
-            (q_hbm, j * (GROUP * HEAD), GROUP * HEAD, 0),
-            (g_hbm, j * (GROUP * HEAD), GROUP * HEAD, GROUP * HEAD),
-            (kv_hbm, j * HEAD, HEAD, 2 * GROUP * HEAD),
-            (kv_hbm, KEY_HEAD_WIDTH + j * HEAD, HEAD, (2 * GROUP + 1) * HEAD),
-        )
+        spans = []
+        for u in range(PAIR):
+            j, to = r * PAIR + u, u * GW
+            spans += [
+                (q_hbm, j * (GROUP * HEAD), GROUP * HEAD, to),
+                (g_hbm, j * (GROUP * HEAD), GROUP * HEAD, to + GROUP * HEAD),
+                (kv_hbm, j * HEAD, HEAD, to + 2 * GROUP * HEAD),
+                (kv_hbm, KEY_HEAD_WIDTH + j * HEAD, HEAD, to + (2 * GROUP + 1) * HEAD),
+            ]
         for i, (src, at, size, to) in enumerate(spans):
             copies.append(
                 pltpu.make_async_copy(
                     src.at[:, pl.ds(pl.multiple_of(at, HEAD), size)],
-                    stage.at[j, :, to : to + size],
-                    load_sem.at[j, i],
+                    stage.at[r, :, to : to + size],
+                    load_sem.at[r, i],
                 )
             )
         return copies
@@ -154,7 +167,7 @@
             copy.start()
         return c
 
-    lax.fori_loop(0, KV_HEADS, start_load, 0)
+    lax.fori_loop(0, ROUNDS, start_load, 0)
     x_copy.start()
     down_copy.start()
     up_copy.start()
@@ -189,9 +202,30 @@
             arr[j, slot] = jnp.zeros(arr.shape[2:], BF16)
         return c
 
-    lax.fori_loop(0, KV_HEADS, clear, 0)
-
-    pl.semaphore_wait(barrier, n_local - 1 + n_node - 1)
+    lax.fori_loop(0, ROUNDS, clear, 0)
+
+    sum_peers = []
+    if factor is not None:
+        core, lx = lax.rem(own_l, 2), own_l // 2
+        y, z = lax.rem(own_n, 2), own_n // 2
+        n_x, n_z = n_local // 2, n_node // 2
+        n_group = 2 * n_x
+        own_g = y * n_x + lx
+        sibling = {"local": lx * 2 + (1 - core), "node": own_n}
+        group = []
+        for o in range(1, n_group):
+            g = lax.rem(own_g + o, n_group)
+            to = {"local": lax.rem(g, n_x) * 2 + core, "node": z * 2 + g // n_x}
+            group.append((g, to))
+        far = []
+        for o in range(1, n_z):
+            t = lax.rem(z + o, n_z)
+            far.append((t, {"local": own_l, "node": t * 2 + y}))
+        sum_peers = [sibling] + [to for _, to in group] + [to for _, to in far]
+        for to in sum_peers:
+            pl.semaphore_signal(barrier, inc=1, device_id=to, device_id_type=pl.DeviceIdType.MESH)
+
+    pl.semaphore_wait(barrier, n_local - 1 + n_node - 1 + len(sum_peers))
 
     def message(j, axis, o, src, dst):
         count, me, base = (n_local, own_l, 0) if axis == "local" else (n_node, own_n, n_local)
@@ -230,13 +264,13 @@
             message(j, axis, o, send.at[j], arr.at[j]).start()
         return carry
 
-    lax.fori_loop(0, KV_HEADS, pack, 0)
+    lax.fori_loop(0, ROUNDS, pack, 0)
     x_copy.wait()
     down_copy.wait()
     down_rows[...] = dot(x_st[...], down_v[...]).astype(BF16)
     send_d[...] = dot(pack_hot[0], down_rows[...]).astype(BF16).reshape(send_d.shape)
     for axis, o in hops:
-        message(KV_HEADS, axis, o, send_d, arr_d).start()
+        message(ROUNDS, axis, o, send_d, arr_d).start()
 
     seg_row = ints[5]
     seg_col = column(seg_row)
@@ -260,6 +294,79 @@
     lax.fori_loop(0, width // HEAD, turn, 0)
     up_copy.wait()
 
+    def remote(src, dst, to_sem, from_sem, to):
+        return pltpu.make_async_remote_copy(
+            src_ref=src,
+            dst_ref=dst,
+            send_sem=to_sem,
+            recv_sem=from_sem,
+            device_id=to,
+            device_id_type=pl.DeviceIdType.MESH,
+        )
+
+    def sums(own_lift):
+        a_rows, b_rows = down_sum.shape[0], up_sum.shape[0]
+
+        def pieces(t, g, at_core):
+            part = (t * 2 + g // n_x) * n_local + lax.rem(g, n_x) * 2 + at_core
+            a = dot(x_turned[pl.ds(pl.multiple_of(part * a_rows, 16), a_rows), :], own_lift)
+            return a, dup_ref[pl.ds(pl.multiple_of(part * b_rows, 16), b_rows), :]
+
+        order = [t for t, _ in far] + [z]
+        copies = []
+        for t in order:
+            for g in range(n_group):
+                a, b = pieces(t, g, 1 - core)
+                send_a[t, g, :a_rows, :] = a.astype(BF16)
+                send_a[t, g, a_rows:, :] = b.astype(BF16)
+            copy = remote(send_a.at[t], recv_a.at[t], sem_a.at[0, t], sem_a.at[1, t], sibling)
+            copy.start()
+            copies.append(copy)
+        for t in order:
+            for g in range(n_group):
+                a, b = pieces(t, g, core)
+                own_part[t, g, :a_rows, :] = a
+                own_part[t, g, a_rows:, :] = b
+        for t, copy in zip(order, copies[:]):
+            copy.wait_recv()
+            for g, to in group:
+                send_b[t, g] = (own_part[t, g] + recv_a[t, g].astype(F32)).astype(BF16)
+                out = remote(
+                    send_b.at[t, g],
+                    recv_b.at[t, own_g],
+                    sem_b.at[0, t, g],
+                    sem_b.at[1, t, own_g],
+                    to,
+                )
+                out.start()
+                copies.append(out)
+            mid[t] = own_part[t, own_g] + recv_a[t, own_g].astype(F32)
+        for i, t in enumerate(order):
+            total = mid[t]
+            for g, to in group:
+                remote(
+                    send_b.at[t, g], recv_b.at[t, g], sem_b.at[0, t, g], sem_b.at[1, t, g], to
+                ).wait_recv()
+                total += recv_b[t, g].astype(F32)
+            if i < len(far):
+                send_c[t] = total.astype(BF16)
+                out = remote(
+                    send_c.at[t], recv_c.at[z], sem_c.at[0, t], sem_c.at[1, z], far[i][1]
+                )
+                out.start()
+                copies.append(out)
+            else:
+                last[...] = total
+        for t, to in far:
+            remote(
+                send_c.at[t], recv_c.at[t], sem_c.at[0, t], sem_c.at[1, t], to
+            ).wait_recv()
+            last[...] += recv_c[t].astype(F32)
+        down_sum[...] = last[:a_rows, :] * factor
+        up_sum[...] = last[a_rows:, :] * factor
+        for copy in copies:
+            copy.wait_send()
+
     scale = 1.0 / math.sqrt(HEAD)
     exp_scale = scale * math.log2(math.e)
     up_row = iota((2 * ADAPTER_RANK, HEAD), 0)
@@ -278,29 +385,35 @@
             ),
         )
 
-    def head(j, carry):
+    def head(r, carry):
         for axis, o in hops:
-            arrival(j, axis, o, send.at[j], arr.at[j]).wait_recv()
-        arrived = arr[j].reshape(entries, GQ)
+            arrival(r, axis, o, send.at[r], arr.at[r]).wait_recv()
+        arrived = arr[r].reshape(entries, GQ)
+        per = GQ // HEAD
         for c in range(4):
-            part = dot(own_hot[...], stage[j, :, c * GQ : (c + 1) * GQ])
+            part = dot(own_hot[...], stage[r, :, c * GQ : (c + 1) * GQ])
             part += dot(arr_hot[c], arrived)
             part = part.astype(BF16)
-            for i in range(3):
-                col = c * 3 + i
+            for i in range(per):
+                u, col = divmod(c * per + i, 2 * GROUP + 2)
                 piece = part[:, i * HEAD : (i + 1) * HEAD]
                 if col >= 2 * GROUP:
-                    kvs[col - 2 * GROUP] = piece
+                    kvs[u, col - 2 * GROUP] = piece
                     continue
                 dst, h = (qs, col) if col < GROUP else (gs, col - GROUP)
                 for b in range(rows // block):
-                    dst[b, h * block : (h + 1) * block, :] = piece[b * block : (b + 1) * block]
+                    dst[u, b, h * block : (h + 1) * block, :] = piece[b * block : (b + 1) * block]
+        for u in range(PAIR):
+            one_head(r * PAIR + u, u)
+        return carry
+
+    def one_head(j, u):
         d_keys = [jnp.zeros((block, HEAD), F32)] * (rows // block)
         d_vals = [jnp.zeros((block, HEAD), F32)] * (rows // block)
         for b in range(rows // block):
             seen = (b + 1) * block
-            scores = dot_t(kvs[0, :seen, :], qs[b])
-            prob_grads = dot_t(kvs[1, :seen, :], gs[b])
+            scores = dot_t(kvs[u, 0, :seen, :], qs[u, b])
+            prob_grads = dot_t(kvs[u, 1, :seen, :], gs[u, b])
             mask = bias[:seen, b * block : (b + 1) * block]
             for h in range(GROUP):
                 cols = slice(h * block, (h + 1) * block)
@@ -310,10 +423,10 @@
                 probs = weights * (1.0 / jnp.sum(weights, axis=0, keepdims=True))
                 prob_grad = prob_grads[:, cols]
                 delta = jnp.sum(probs * prob_grad, axis=0, keepdims=True)
-                probs_s[b, :seen, cols] = probs.astype(BF16)
-                grads_s[b, :seen, cols] = (probs * (prob_grad - delta)).astype(BF16)
-            d_val = dot(probs_s[b, :seen, :], gs[b])
-            d_key = dot(grads_s[b, :seen, :], qs[b])
+                probs_s[u, b, :seen, cols] = probs.astype(BF16)
+                grads_s[u, b, :seen, cols] = (probs * (prob_grad - delta)).astype(BF16)
+            d_val = dot(probs_s[u, b, :seen, :], gs[u, b])
+            d_key = dot(grads_s[u, b, :seen, :], qs[u, b])
             for t in range(b + 1):
                 d_vals[t] += d_val[t * block : (t + 1) * block]
                 d_keys[t] += d_key[t * block : (t + 1) * block]
@@ -331,17 +444,16 @@
         up_key = jnp.where(up_row < ADAPTER_RANK, up, 0.0).astype(BF16)
         up_val = jnp.where(up_row < ADAPTER_RANK, 0.0, up).astype(BF16)
         lift[...] += dot_t(key_low, up_key) + dot_t(val_low, up_val)
-        return carry
-
-    lax.fori_loop(0, KV_HEADS, head, 0)
+
+    lax.fori_loop(0, ROUNDS, head, 0)
 
     lift_low = lift[...].astype(BF16)
     send_l[...] = dot_l(arr_hot[0], lift_low).astype(BF16).reshape(send_l.shape)
     for axis, o in hops:
-        message(KV_HEADS + 1, axis, o, send_l, arr_l).start()
+        message(ROUNDS + 1, axis, o, send_l, arr_l).start()
 
     for axis, o in hops:
-        arrival(KV_HEADS, axis, o, send_d, arr_d).wait_recv()
+        arrival(ROUNDS, axis, o, send_d, arr_d).wait_recv()
     down_out = dot(own_hot[...], down_rows[...])
     down_out += dot(arr_hot[0], arr_d[...].reshape(entries, HEAD))
     down_low = down_out.astype(BF16)
@@ -359,26 +471,33 @@
 
     own_lift = dot_l(own_hot[...], lift_low)
     for axis, o in hops:
-        arrival(KV_HEADS + 1, axis, o, send_l, arr_l).wait_recv()
+        arrival(ROUNDS + 1, axis, o, send_l, arr_l).wait_recv()
     own_lift += dot_l(pack_hot[0], arr_l[...].reshape(entries, HEAD))
     own_lift = own_lift.astype(BF16)
-    span = width // 8
-    for c in range(8):
-        ddown_ref[c * span : (c + 1) * span, :] = dot(
-            x_turned[c * span : (c + 1) * span, :], own_lift
-        )
+    if factor is None:
+        span = width // 8
+        for c in range(8):
+            at = slice(c * span, (c + 1) * span)
+            ddown_ref[at, :] = dot(x_turned[at, :], own_lift)
+    else:
+        sums(own_lift)
 
     def finish(j, carry):
         for copy in cot_copies(j):
             copy.wait()
+        return carry
+
+    lax.fori_loop(0, KV_HEADS, finish, 0)
+
+    def sent(r, carry):
         for axis, o in hops:
-            message(j, axis, o, send.at[j], arr.at[j]).wait_send()
+            message(r, axis, o, send.at[r], arr.at[r]).wait_send()
         return carry
 
-    lax.fori_loop(0, KV_HEADS, finish, 0)
+    lax.fori_loop(0, ROUNDS, sent, 0)
     for axis, o in hops:
-        message(KV_HEADS, axis, o, send_d, arr_d).wait_send()
-        message(KV_HEADS + 1, axis, o, send_l, arr_l).wait_send()
+        message(ROUNDS, axis, o, send_d, arr_d).wait_send()
+        message(ROUNDS + 1, axis, o, send_l, arr_l).wait_send()
 
 
 def sum_kernel(
@@ -567,27 +686,52 @@
     entries = peers * CHUNK
     vmem = pl.BlockSpec(memory_space=pltpu.VMEM)
     hbm = pl.BlockSpec(memory_space=pl.ANY)
+    n_dev = n_local * n_node
+    wide = 2 * ADAPTER_RANK
+    factor = 1.0 / math.sqrt(rows * n_dev)
+    a_rows, b_rows = width // n_dev, KEY_HEAD_WIDTH // n_dev
+    fused = a_rows % 16 == 0 and b_rows % 16 == 0
+    shrink = n_dev if fused else 1
+    extra = []
+    if fused:
+        n_z, n_group, size = n_node // 2, n_local, a_rows + b_rows
+        slab = (n_z, n_group, size, wide)
+        extra = [
+            pltpu.VMEM((KEY_HEAD_WIDTH, wide), F32),
+            pltpu.VMEM(slab, BF16),
+            pltpu.VMEM(slab, BF16),
+            pltpu.VMEM(slab, BF16),
+            pltpu.VMEM(slab, BF16),
+            pltpu.VMEM((n_z, size, wide), BF16),
+            pltpu.VMEM((n_z, size, wide), BF16),
+            pltpu.VMEM(slab, F32),
+            pltpu.VMEM((n_z, size, wide), F32),
+            pltpu.VMEM((size, wide), F32),
+            pltpu.SemaphoreType.DMA((2, n_z)),
+            pltpu.SemaphoreType.DMA((2, n_z, n_group)),
+            pltpu.SemaphoreType.DMA((2, n_z)),
+        ]
     cotangent, down_grad, up_grad = pl.pallas_call(
-        functools.partial(main_kernel, n_local, n_node),
+        functools.partial(main_kernel, n_local, n_node, factor if fused else None),
         out_shape=(
             jax.ShapeDtypeStruct((rows, 2 * KEY_HEAD_WIDTH), BF16),
-            jax.ShapeDtypeStruct((width, 2 * ADAPTER_RANK), F32),
-            jax.ShapeDtypeStruct((KEY_HEAD_WIDTH, 2 * ADAPTER_RANK), F32),
+            jax.ShapeDtypeStruct((width // shrink, wide), F32),
+            jax.ShapeDtypeStruct((KEY_HEAD_WIDTH // shrink, wide), F32),
         ),
         in_specs=[hbm] * 12,
         out_specs=(hbm, vmem, vmem),
         scratch_shapes=[
             pltpu.VMEM((6, 1, rows), jnp.int32),
             pltpu.VMEM(adapter_up.shape, BF16),
-            pltpu.VMEM((KV_HEADS, rows, GW), BF16),
+            pltpu.VMEM((ROUNDS, rows, PAIR * GW), BF16),
             pltpu.VMEM((rows, width), BF16),
             pltpu.VMEM((width, rows), BF16),
             pltpu.VMEM((width, 2 * ADAPTER_RANK), BF16),
             pltpu.VMEM((rows, 2 * ADAPTER_RANK), BF16),
-            pltpu.VMEM((KV_HEADS, peers, CHUNK, GQ), BF16),
+            pltpu.VMEM((ROUNDS, peers, CHUNK, GQ), BF16),
             pltpu.VMEM((peers, CHUNK, 2 * ADAPTER_RANK), BF16),
             pltpu.VMEM((peers, CHUNK, 2 * ADAPTER_RANK), BF16),
-            pltpu.VMEM((KV_HEADS, peers, CHUNK, GQ), BF16),
+            pltpu.VMEM((ROUNDS, peers, CHUNK, GQ), BF16),
             pltpu.VMEM((peers, CHUNK, 2 * ADAPTER_RANK), BF16),
             pltpu.VMEM((peers, CHUNK, 2 * ADAPTER_RANK), BF16),
             pltpu.VMEM((4, entries, rows), BF16),
@@ -596,27 +740,29 @@
             pltpu.VMEM((rows, rows), F32),
             pltpu.VMEM((rows, HEAD), F32),
             pltpu.VMEM((rows, HEAD), F32),
-            pltpu.VMEM((rows // HEAD, GROUP * HEAD, HEAD), BF16),
-            pltpu.VMEM((rows // HEAD, GROUP * HEAD, HEAD), BF16),
-            pltpu.VMEM((2, rows, HEAD), BF16),
-            pltpu.VMEM((rows // HEAD, rows, GROUP * HEAD), BF16),
-            pltpu.VMEM((rows // HEAD, rows, GROUP * HEAD), BF16),
+            pltpu.VMEM((PAIR, rows // HEAD, GROUP * HEAD, HEAD), BF16),
+            pltpu.VMEM((PAIR, rows // HEAD, GROUP * HEAD, HEAD), BF16),
+            pltpu.VMEM((PAIR, 2, rows, HEAD), BF16),
+            pltpu.VMEM((PAIR, rows // HEAD, rows, GROUP * HEAD), BF16),
+            pltpu.VMEM((PAIR, rows // HEAD, rows, GROUP * HEAD), BF16),
             pltpu.VMEM((KV_HEADS, rows, HEAD), BF16),
             pltpu.VMEM((KV_HEADS, rows, HEAD), BF16),
             pltpu.VMEM((rows, 2 * ADAPTER_RANK), F32),
             pltpu.SemaphoreType.DMA((6,)),
-            pltpu.SemaphoreType.DMA((KV_HEADS, 4)),
+            pltpu.SemaphoreType.DMA((ROUNDS, 4 * PAIR)),
             pltpu.SemaphoreType.DMA((3,)),
             pltpu.SemaphoreType.DMA((KV_HEADS, 2)),
-            pltpu.SemaphoreType.DMA((KV_HEADS + 2, peers)),
-            pltpu.SemaphoreType.DMA((KV_HEADS + 2, peers)),
+            pltpu.SemaphoreType.DMA((ROUNDS + 2, peers)),
+            pltpu.SemaphoreType.DMA((ROUNDS + 2, peers)),
+            *extra,
         ],
         compiler_params=pltpu.CompilerParams(
-            collective_id=0, has_side_effects=True, vmem_limit_bytes=48 * 2**20
+            collective_id=0, has_side_effects=True, vmem_limit_bytes=60 * 2**20
         ),
         name="exchange_attention",
     )(*args)
-    factor = 1.0 / math.sqrt(rows * n_local * n_node)
+    if fused:
+        return cotangent, down_grad, up_grad
     down_sum, up_sum = factor_sums(n_local, n_node, factor, down_grad, up_grad)
     return cotangent, down_sum, up_sum
 

time: 73.6 us -> 59.4 us (0.81)
  Pallas kernels: 61.1 us -> 53.4 us
  local copies, waits for them, and re-layouts: 11.5 us -> 5.15 us
    pallas_call x2 -> x1, Pallas kernels: 61.1 us -> 53.4 us  [local(): pl.pallas_call(functools.partial(main_kernel, n_local, n_node, factor if...]
    unnamed x23 -> x3, local copies, waits for them, and re-layouts: 11.5 us -> 5.15 us
where the time goes in v3:
time: 59.4 us; the launch traced here: 59.2 us
  Pallas kernels  53.4 us (90%)
  local copies, waits for them, and re-layouts  5.15 us (9%)
  between operations  0.64 us (1%)
    pallas_call x1, Pallas kernels, local(): pl.pallas_call(functools.partial(main_kernel, n_local, n_node, factor if...  53.4 us
    unnamed x3, local copies, waits for them, and re-layouts  5.15 us

profile of v3, /device:TPU:0, one launch (start us, length us, event | category | flops | bytes accessed | tf_op | source)
XLA Modules:
  0.0 59.2 jit_solution(7677399271309658773)
XLA Ops:
  0.6 53.4 %exchange_attention.1 = (bf16[256,2048]{1,0:T(8,128)(2,1)}, f32[160,128]{1,0:T(8,128)}, f32[32,128]{1,0:T(8,128)}) custom-call(bf16[256,5120]{1,0:T(8,128)(2,1)} %x_hbm.1, bf16[256,5120]{1,0:T(8,128)(2,1)} %q_hbm.1, bf16[256,2048]{1,0:T(8,128)(2,1)} %kv_hbm.1, bf16[256,5120]{1,0:T(8,128)(2,1)} %g_hbm.1, bf16[5120,128]{1,0:T(8,128)(2,1)} %down_hbm.1, ...), custom_call_target="tpu_custom_call" | custom-call | tf_op jit(solution)/shard_map/exchange_attention/pallas_call | solution.py:714
  54.0 2.3 %copy.18 = bf16[256,2048]{1,0:T(8,128)(2,1)} copy(bf16[256,2048]{1,0:T(8,128)(2,1)} %get-tuple-element.6) | data formatting | bytes 2097152
  56.3 1.5 %copy.19 = f32[160,128]{1,0:T(8,128)} copy(f32[160,128]{1,0:T(8,128)} %get-tuple-element.7) | data formatting | bytes 163840
  57.8 1.3 %copy.20 = f32[32,128]{1,0:T(8,128)} copy(f32[32,128]{1,0:T(8,128)} %get-tuple-element.8) | data formatting | bytes 32768

commit v4 on v3

--- a/solution.py
+++ b/solution.py
@@ -167,10 +167,7 @@
             copy.start()
         return c
 
-    lax.fori_loop(0, ROUNDS, start_load, 0)
-    x_copy.start()
-    down_copy.start()
-    up_copy.start()
+    lax.fori_loop(0, 2, start_load, 0)
     for copy in int_copies:
         copy.wait()
     near_bin, near_off, far_bin, far_off = ints[0], ints[1], ints[2], ints[3]
@@ -183,15 +180,9 @@
         jnp.where(moved_out, (n_local + far_bin) * CAP + far_off, -1),
     )
     a_sub = iota((entries, rows), 0)
-    hit = code == (a_sub // CHUNK) * CAP + a_sub % CAP
+    hit = code == (a_sub >> 4) * CAP + (a_sub & 3)
     for c in range(4):
-        pack_hot[c] = jnp.where(hit & ((a_sub // CAP) % 4 == c), 1.0, 0.0).astype(BF16)
-    pick = column(ints[4])
-    own_hot[...] = jnp.where(pick == iota((rows, rows), 1), 1.0, 0.0).astype(BF16)
-    a_lane = iota((rows, entries), 1)
-    got = pick == rows + (a_lane // CHUNK) * CAP + a_lane % CAP
-    for c in range(4):
-        arr_hot[c] = jnp.where(got & ((a_lane // CAP) % 4 == c), 1.0, 0.0).astype(BF16)
+        pack_hot[c] = jnp.where(hit & (((a_sub >> 2) & 3) == c), 1.0, 0.0).astype(BF16)
 
     for slot in (own_l, n_local + own_n):
         arr_d[slot] = jnp.zeros(arr_d.shape[1:], BF16)
@@ -256,6 +247,17 @@
     def pack(j, carry):
         for copy in load(j):
             copy.wait()
+
+        @pl.when(j + 2 < ROUNDS)
+        def _():
+            start_load(j + 2, 0)
+
+        @pl.when(j + 2 == ROUNDS)
+        def _():
+            x_copy.start()
+            down_copy.start()
+            up_copy.start()
+
         total = dot(pack_hot[0], stage[j, :, 0:GQ])
         for c in range(1, 4):
             total += dot(pack_hot[c], stage[j, :, c * GQ : (c + 1) * GQ])
@@ -265,6 +267,14 @@
         return carry
 
     lax.fori_loop(0, ROUNDS, pack, 0)
+
+    pick = column(ints[4])
+    own_hot[...] = jnp.where(pick == iota((rows, rows), 1), 1.0, 0.0).astype(BF16)
+    a_lane = iota((rows, entries), 1)
+    got = pick == rows + (a_lane >> 4) * CAP + (a_lane & 3)
+    for c in range(4):
+        arr_hot[c] = jnp.where(got & (((a_lane >> 2) & 3) == c), 1.0, 0.0).astype(BF16)
+
     x_copy.wait()
     down_copy.wait()
     down_rows[...] = dot(x_st[...], down_v[...]).astype(BF16)
@@ -307,30 +317,31 @@
     def sums(own_lift):
         a_rows, b_rows = down_sum.shape[0], up_sum.shape[0]
 
-        def pieces(t, g, at_core):
+        slab_rows = 2 * n_group * a_rows
+
+        def up_piece(t, g, at_core):
             part = (t * 2 + g // n_x) * n_local + lax.rem(g, n_x) * 2 + at_core
-            a = dot(x_turned[pl.ds(pl.multiple_of(part * a_rows, 16), a_rows), :], own_lift)
-            return a, dup_ref[pl.ds(pl.multiple_of(part * b_rows, 16), b_rows), :]
+            return dup_ref[pl.ds(pl.multiple_of(part * b_rows, 16), b_rows), :]
 
         order = [t for t, _ in far] + [z]
         copies = []
         for t in order:
+            slab = dot(x_turned[pl.ds(pl.multiple_of(t * slab_rows, 16), slab_rows), :], own_lift)
+            own_part[t] = slab.reshape(2 * n_group, a_rows, slab.shape[1])
             for g in range(n_group):
-                a, b = pieces(t, g, 1 - core)
-                send_a[t, g, :a_rows, :] = a.astype(BF16)
-                send_a[t, g, a_rows:, :] = b.astype(BF16)
+                send_a[t, g, :a_rows, :] = own_part[t, g * 2 + 1 - core].astype(BF16)
+                send_a[t, g, a_rows:, :] = up_piece(t, g, 1 - core).astype(BF16)
             copy = remote(send_a.at[t], recv_a.at[t], sem_a.at[0, t], sem_a.at[1, t], sibling)
             copy.start()
             copies.append(copy)
-        for t in order:
-            for g in range(n_group):
-                a, b = pieces(t, g, core)
-                own_part[t, g, :a_rows, :] = a
-                own_part[t, g, a_rows:, :] = b
         for t, copy in zip(order, copies[:]):
             copy.wait_recv()
             for g, to in group:
-                send_b[t, g] = (own_part[t, g] + recv_a[t, g].astype(F32)).astype(BF16)
+                got = recv_a[t, g].astype(F32)
+                a = own_part[t, g * 2 + core] + got[:a_rows]
+                b = up_piece(t, g, core) + got[a_rows:]
+                send_b[t, g, :a_rows, :] = a.astype(BF16)
+                send_b[t, g, a_rows:, :] = b.astype(BF16)
                 out = remote(
                     send_b.at[t, g],
                     recv_b.at[t, own_g],
@@ -340,7 +351,9 @@
                 )
                 out.start()
                 copies.append(out)
-            mid[t] = own_part[t, own_g] + recv_a[t, own_g].astype(F32)
+            got = recv_a[t, own_g].astype(F32)
+            mid[t, :a_rows, :] = own_part[t, own_g * 2 + core] + got[:a_rows]
+            mid[t, a_rows:, :] = up_piece(t, own_g, core) + got[a_rows:]
         for i, t in enumerate(order):
             total = mid[t]
             for g, to in group:
@@ -679,6 +692,34 @@
     return a_out[:a_size], b_out[:b_size]
 
 
+def hand_out_kernel(parts, c_in, a_in, b_in, c_out, a_out, b_out, sem):
+    step = c_in.shape[0] // parts
+    spans = [(c_in, c_out, i * step, step) for i in range(parts)]
+    spans += [(a_in, a_out, 0, a_in.shape[0]), (b_in, b_out, 0, b_in.shape[0])]
+    copies = [
+        pltpu.make_async_copy(src.at[at : at + n], dst.at[at : at + n], sem.at[i])
+        for i, (src, dst, at, n) in enumerate(spans)
+    ]
+    for copy in copies:
+        copy.start()
+    for copy in copies:
+        copy.wait()
+
+
+def hand_out(*arrays):
+    parts = 4
+    hbm = pl.BlockSpec(memory_space=pl.ANY)
+    return pl.pallas_call(
+        functools.partial(hand_out_kernel, parts),
+        out_shape=tuple(jax.ShapeDtypeStruct(v.shape, v.dtype) for v in arrays),
+        in_specs=[hbm] * 3,
+        out_specs=(hbm,) * 3,
+        scratch_shapes=[pltpu.SemaphoreType.DMA((parts + 2,))],
+        compiler_params=pltpu.CompilerParams(vmem_limit_bytes=60 * 2**20),
+        name="hand_out",
+    )(*arrays)
+
+
 def local(n_local, n_node, *args):
     activations, queries, rotated_key_value, attention_out_grad, adapter_down, adapter_up = args[:6]
     rows, width = activations.shape
@@ -704,7 +745,7 @@
             pltpu.VMEM(slab, BF16),
             pltpu.VMEM((n_z, size, wide), BF16),
             pltpu.VMEM((n_z, size, wide), BF16),
-            pltpu.VMEM(slab, F32),
+            pltpu.VMEM((n_z, 2 * n_group, a_rows, wide), F32),
             pltpu.VMEM((n_z, size, wide), F32),
             pltpu.VMEM((size, wide), F32),
             pltpu.SemaphoreType.DMA((2, n_z)),
@@ -762,7 +803,7 @@
         name="exchange_attention",
     )(*args)
     if fused:
-        return cotangent, down_grad, up_grad
+        return hand_out(cotangent, down_grad, up_grad)
     down_sum, up_sum = factor_sums(n_local, n_node, factor, down_grad, up_grad)
     return cotangent, down_sum, up_sum
 

time: 59.4 us -> 90.5 us (1.52)
  Pallas kernels: 53.4 us -> 89.7 us
  local copies, waits for them, and re-layouts: 5.15 us -> 0 us
    pallas_call x0 -> x1, Pallas kernels: none -> 35.9 us  [hand_out(): pl.pallas_call(functools.partial(hand_out_kernel, parts), out_shape=tuple...]
    unnamed x3 -> x0, local copies, waits for them, and re-layouts: 5.15 us -> none
where the time goes in v4:
time: 90.5 us; the launch traced here: 90.3 us
  Pallas kernels  89.7 us (99%)
    pallas_call x1, Pallas kernels, local(): pl.pallas_call(functools.partial(main_kernel, n_local, n_node, factor if...  53.8 us
    pallas_call x1, Pallas kernels, hand_out(): pl.pallas_call(functools.partial(hand_out_kernel, parts), out_shape=tuple...  35.9 us

profile of v4, /device:TPU:0, one launch (start us, length us, event | category | flops | bytes accessed | tf_op | source)
XLA Modules:
  0.0 90.3 jit_solution(1119507631735426832)
XLA Ops:
  0.6 53.8 %exchange_attention.1 = (bf16[256,2048]{1,0:T(8,128)(2,1)}, f32[160,128]{1,0:T(8,128)}, f32[32,128]{1,0:T(8,128)}) custom-call(bf16[256,5120]{1,0:T(8,128)(2,1)} %x_hbm.1, bf16[256,5120]{1,0:T(8,128)(2,1)} %q_hbm.1, bf16[256,2048]{1,0:T(8,128)(2,1)} %kv_hbm.1, bf16[256,5120]{1,0:T(8,128)(2,1)} %g_hbm.1, bf16[5120,128]{1,0:T(8,128)(2,1)} %down_hbm.1, ...), custom_call_target="tpu_custom_call" | custom-call | tf_op jit(solution)/shard_map/exchange_attention/pallas_call | solution.py:755
  54.4 35.9 %hand_out.1 = (bf16[256,2048]{1,0:T(8,128)(2,1)}, f32[160,128]{1,0:T(8,128)}, f32[32,128]{1,0:T(8,128)}) custom-call(bf16[256,2048]{1,0:T(8,128)(2,1)} %get-tuple-element.6.c_in, f32[160,128]{1,0:T(8,128)} %get-tuple-element.7.a_in, f32[32,128]{1,0:T(8,128)} %get-tuple-element.8.b_in), custom_call_target="tpu_custom_call" | custom-call | tf_op jit(solution)/shard_map/hand_out/pallas_call | solution.py:712

commit v5 on v4

--- a/solution.py
+++ b/solution.py
@@ -87,8 +87,7 @@
         arr_d,
         arr_l,
         pack_hot,
-        own_hot,
-        arr_hot,
+        slot_hot,
         bias,
         cos_v,
         sin_v,
@@ -106,7 +105,7 @@
         out_sem,
         send_sem,
         recv_sem,
-    ) = rest[2:35]
+    ) = rest[2:34]
     rows = x_st.shape[0]
     width = x_st.shape[1]
     block = HEAD
@@ -182,7 +181,7 @@
     a_sub = iota((entries, rows), 0)
     hit = code == (a_sub >> 4) * CAP + (a_sub & 3)
     for c in range(4):
-        pack_hot[c] = jnp.where(hit & (((a_sub >> 2) & 3) == c), 1.0, 0.0).astype(BF16)
+        pack_hot[:, c * rows : (c + 1) * rows] = jnp.where(hit & (((a_sub >> 2) & 3) == c), 1.0, 0.0).astype(BF16)
 
     for slot in (own_l, n_local + own_n):
         arr_d[slot] = jnp.zeros(arr_d.shape[1:], BF16)
@@ -258,9 +257,8 @@
             down_copy.start()
             up_copy.start()
 
-        total = dot(pack_hot[0], stage[j, :, 0:GQ])
-        for c in range(1, 4):
-            total += dot(pack_hot[c], stage[j, :, c * GQ : (c + 1) * GQ])
+        quarters = [stage[j, :, c * GQ : (c + 1) * GQ] for c in range(4)]
+        total = dot(pack_hot[...], jnp.concatenate(quarters, axis=0))
         send[j] = total.astype(BF16).reshape(peers, CHUNK, GQ)
         for axis, o in hops:
             message(j, axis, o, send.at[j], arr.at[j]).start()
@@ -269,16 +267,17 @@
     lax.fori_loop(0, ROUNDS, pack, 0)
 
     pick = column(ints[4])
-    own_hot[...] = jnp.where(pick == iota((rows, rows), 1), 1.0, 0.0).astype(BF16)
+    own_picks = jnp.where(pick == iota((rows, rows), 1), 1.0, 0.0).astype(BF16)
     a_lane = iota((rows, entries), 1)
     got = pick == rows + (a_lane >> 4) * CAP + (a_lane & 3)
     for c in range(4):
-        arr_hot[c] = jnp.where(got & (((a_lane >> 2) & 3) == c), 1.0, 0.0).astype(BF16)
+        slot_hot[c, :, :rows] = own_picks
+        slot_hot[c, :, rows:] = jnp.where(got & (((a_lane >> 2) & 3) == c), 1.0, 0.0).astype(BF16)
 
     x_copy.wait()
     down_copy.wait()
     down_rows[...] = dot(x_st[...], down_v[...]).astype(BF16)
-    send_d[...] = dot(pack_hot[0], down_rows[...]).astype(BF16).reshape(send_d.shape)
+    send_d[...] = dot(pack_hot[:, :rows], down_rows[...]).astype(BF16).reshape(send_d.shape)
     for axis, o in hops:
         message(ROUNDS, axis, o, send_d, arr_d).start()
 
@@ -404,9 +403,8 @@
         arrived = arr[r].reshape(entries, GQ)
         per = GQ // HEAD
         for c in range(4):
-            part = dot(own_hot[...], stage[r, :, c * GQ : (c + 1) * GQ])
-            part += dot(arr_hot[c], arrived)
-            part = part.astype(BF16)
+            listed = jnp.concatenate([stage[r, :, c * GQ : (c + 1) * GQ], arrived], axis=0)
+            part = dot(slot_hot[c], listed).astype(BF16)
             for i in range(per):
                 u, col = divmod(c * per + i, 2 * GROUP + 2)
                 piece = part[:, i * HEAD : (i + 1) * HEAD]
@@ -416,17 +414,20 @@
                 dst, h = (qs, col) if col < GROUP else (gs, col - GROUP)
                 for b in range(rows // block):
                     dst[u, b, h * block : (h + 1) * block, :] = piece[b * block : (b + 1) * block]
-        for u in range(PAIR):
-            one_head(r * PAIR + u, u)
-        return carry
-
-    def one_head(j, u):
-        d_keys = [jnp.zeros((block, HEAD), F32)] * (rows // block)
-        d_vals = [jnp.zeros((block, HEAD), F32)] * (rows // block)
-        for b in range(rows // block):
+        tasks = [(u, b) for b in range(rows // block) for u in range(PAIR)]
+        d_keys = [[jnp.zeros((block, HEAD), F32)] * (rows // block) for _ in range(PAIR)]
+        d_vals = [[jnp.zeros((block, HEAD), F32)] * (rows // block) for _ in range(PAIR)]
+
+        def products(u, b):
             seen = (b + 1) * block
-            scores = dot_t(kvs[u, 0, :seen, :], qs[u, b])
-            prob_grads = dot_t(kvs[u, 1, :seen, :], gs[u, b])
+            return dot_t(kvs[u, 0, :seen, :], qs[u, b]), dot_t(kvs[u, 1, :seen, :], gs[u, b])
+
+        ahead = products(*tasks[0])
+        for i, (u, b) in enumerate(tasks):
+            scores, prob_grads = ahead
+            if i + 1 < len(tasks):
+                ahead = products(*tasks[i + 1])
+            seen = (b + 1) * block
             mask = bias[:seen, b * block : (b + 1) * block]
             for h in range(GROUP):
                 cols = slice(h * block, (h + 1) * block)
@@ -441,34 +442,38 @@
             d_val = dot(probs_s[u, b, :seen, :], gs[u, b])
             d_key = dot(grads_s[u, b, :seen, :], qs[u, b])
             for t in range(b + 1):
-                d_vals[t] += d_val[t * block : (t + 1) * block]
-                d_keys[t] += d_key[t * block : (t + 1) * block]
-        d_key = jnp.concatenate(d_keys, axis=0)
-        d_val = jnp.concatenate(d_vals, axis=0)
-        d_key = d_key * scale
-        d_key = d_key * cos_v[...] + pltpu.roll(d_key, HEAD // 2, 1) * sin_v[...]
-        key_low = d_key.astype(BF16)
-        val_low = d_val.astype(BF16)
-        keys_out[j] = key_low
-        vals_out[j] = val_low
-        for copy in cot_copies(j):
-            copy.start()
-        up = up_ref[:, pl.ds(pl.multiple_of(j * HEAD, HEAD), HEAD)].astype(F32)
-        up_key = jnp.where(up_row < ADAPTER_RANK, up, 0.0).astype(BF16)
-        up_val = jnp.where(up_row < ADAPTER_RANK, 0.0, up).astype(BF16)
-        lift[...] += dot_t(key_low, up_key) + dot_t(val_low, up_val)
+                d_vals[u][t] += d_val[t * block : (t + 1) * block]
+                d_keys[u][t] += d_key[t * block : (t + 1) * block]
+        total = lift[...]
+        for u in range(PAIR):
+            j = r * PAIR + u
+            d_key = jnp.concatenate(d_keys[u], axis=0) * scale
+            d_key = d_key * cos_v[...] + pltpu.roll(d_key, HEAD // 2, 1) * sin_v[...]
+            key_low = d_key.astype(BF16)
+            val_low = jnp.concatenate(d_vals[u], axis=0).astype(BF16)
+            keys_out[j] = key_low
+            vals_out[j] = val_low
+            up = up_ref[:, pl.ds(pl.multiple_of(j * HEAD, HEAD), HEAD)].astype(F32)
+            up_key = jnp.where(up_row < ADAPTER_RANK, up, 0.0).astype(BF16)
+            up_val = jnp.where(up_row < ADAPTER_RANK, 0.0, up).astype(BF16)
+            total += dot_t(key_low, up_key) + dot_t(val_low, up_val)
+        lift[...] = total
+        for u in range(PAIR):
+            for copy in cot_copies(r * PAIR + u):
+                copy.start()
+        return carry
 
     lax.fori_loop(0, ROUNDS, head, 0)
 
     lift_low = lift[...].astype(BF16)
-    send_l[...] = dot_l(arr_hot[0], lift_low).astype(BF16).reshape(send_l.shape)
+    send_l[...] = dot_l(slot_hot[0, :, rows:], lift_low).astype(BF16).reshape(send_l.shape)
     for axis, o in hops:
         message(ROUNDS + 1, axis, o, send_l, arr_l).start()
 
     for axis, o in hops:
         arrival(ROUNDS, axis, o, send_d, arr_d).wait_recv()
-    down_out = dot(own_hot[...], down_rows[...])
-    down_out += dot(arr_hot[0], arr_d[...].reshape(entries, HEAD))
+    down_out = dot(slot_hot[0, :, :rows], down_rows[...])
+    down_out += dot(slot_hot[0, :, rows:], arr_d[...].reshape(entries, HEAD))
     down_low = down_out.astype(BF16)
     down_lane = iota((HEAD, 2 * ADAPTER_RANK), 1) < ADAPTER_RANK
 
@@ -482,10 +487,10 @@
 
     lax.fori_loop(0, KV_HEADS, up_grad, 0)
 
-    own_lift = dot_l(own_hot[...], lift_low)
+    own_lift = dot_l(slot_hot[0, :, :rows], lift_low)
     for axis, o in hops:
         arrival(ROUNDS + 1, axis, o, send_l, arr_l).wait_recv()
-    own_lift += dot_l(pack_hot[0], arr_l[...].reshape(entries, HEAD))
+    own_lift += dot_l(pack_hot[:, :rows], arr_l[...].reshape(entries, HEAD))
     own_lift = own_lift.astype(BF16)
     if factor is None:
         span = width // 8
@@ -692,17 +697,21 @@
     return a_out[:a_size], b_out[:b_size]
 
 
-def hand_out_kernel(parts, c_in, a_in, b_in, c_out, a_out, b_out, sem):
+def hand_out_kernel(parts, c_in, a_in, b_in, c_out, a_out, b_out, c_v, a_v, b_v, sem):
     step = c_in.shape[0] // parts
-    spans = [(c_in, c_out, i * step, step) for i in range(parts)]
-    spans += [(a_in, a_out, 0, a_in.shape[0]), (b_in, b_out, 0, b_in.shape[0])]
-    copies = [
-        pltpu.make_async_copy(src.at[at : at + n], dst.at[at : at + n], sem.at[i])
-        for i, (src, dst, at, n) in enumerate(spans)
-    ]
-    for copy in copies:
+    spans = [(c_in, c_v, c_out, i * step, step) for i in range(parts)]
+    spans += [(a_in, a_v, a_out, 0, a_in.shape[0]), (b_in, b_v, b_out, 0, b_in.shape[0])]
+    loads, stores = [], []
+    for i, (src, mid, dst, at, n) in enumerate(spans):
+        rows = slice(at, at + n)
+        loads.append(pltpu.make_async_copy(src.at[rows], mid.at[rows], sem.at[0, i]))
+        stores.append(pltpu.make_async_copy(mid.at[rows], dst.at[rows], sem.at[1, i]))
+    for copy in loads:
         copy.start()
-    for copy in copies:
+    for first, second in zip(loads, stores):
+        first.wait()
+        second.start()
+    for copy in stores:
         copy.wait()
 
 
@@ -714,7 +723,8 @@
         out_shape=tuple(jax.ShapeDtypeStruct(v.shape, v.dtype) for v in arrays),
         in_specs=[hbm] * 3,
         out_specs=(hbm,) * 3,
-        scratch_shapes=[pltpu.SemaphoreType.DMA((parts + 2,))],
+        scratch_shapes=[pltpu.VMEM(v.shape, v.dtype) for v in arrays]
+        + [pltpu.SemaphoreType.DMA((2, parts + 2))],
         compiler_params=pltpu.CompilerParams(vmem_limit_bytes=60 * 2**20),
         name="hand_out",
     )(*arrays)
@@ -775,9 +785,8 @@
             pltpu.VMEM((ROUNDS, peers, CHUNK, GQ), BF16),
             pltpu.VMEM((peers, CHUNK, 2 * ADAPTER_RANK), BF16),
             pltpu.VMEM((peers, CHUNK, 2 * ADAPTER_RANK), BF16),
-            pltpu.VMEM((4, entries, rows), BF16),
-            pltpu.VMEM((rows, rows), BF16),
-            pltpu.VMEM((4, rows, entries), BF16),
+            pltpu.VMEM((entries, 4 * rows), BF16),
+            pltpu.VMEM((4, rows, rows + entries), BF16),
             pltpu.VMEM((rows, rows), F32),
             pltpu.VMEM((rows, HEAD), F32),
             pltpu.VMEM((rows, HEAD), F32),

time: 90.5 us -> 55.7 us (0.62)
  Pallas kernels: 89.7 us -> 54.9 us
    pallas_call x1, Pallas kernels: 35.9 us -> 2.04 us  [hand_out(): pl.pallas_call(functools.partial(hand_out_kernel, parts), out_shape=tuple...]
    pallas_call x1, Pallas kernels: 53.8 us -> 52.8 us  [local(): pl.pallas_call(functools.partial(main_kernel, n_local, n_node, factor if...]
where the time goes in v5:
time: 55.7 us; the launch traced here: 55.5 us
  Pallas kernels  54.9 us (99%)
  between operations  0.64 us (1%)
    pallas_call x1, Pallas kernels, local(): pl.pallas_call(functools.partial(main_kernel, n_local, n_node, factor if...  52.8 us
    pallas_call x1, Pallas kernels, hand_out(): pl.pallas_call(functools.partial(hand_out_kernel, parts), out_shape=tuple...  2.04 us

profile of v5, /device:TPU:0, one launch (start us, length us, event | category | flops | bytes accessed | tf_op | source)
XLA Modules:
  0.0 55.5 jit_solution(6834292682304094000)
XLA Ops:
  0.6 52.8 %exchange_attention.1 = (bf16[256,2048]{1,0:T(8,128)(2,1)}, f32[160,128]{1,0:T(8,128)}, f32[32,128]{1,0:T(8,128)}) custom-call(bf16[256,5120]{1,0:T(8,128)(2,1)} %x_hbm.1, bf16[256,5120]{1,0:T(8,128)(2,1)} %q_hbm.1, bf16[256,2048]{1,0:T(8,128)(2,1)} %kv_hbm.1, bf16[256,5120]{1,0:T(8,128)(2,1)} %g_hbm.1, bf16[5120,128]{1,0:T(8,128)(2,1)} %down_hbm.1, ...), custom_call_target="tpu_custom_call" | custom-call | tf_op jit(solution)/shard_map/exchange_attention/pallas_call | solution.py:765
  53.5 2.0 %hand_out.1 = (bf16[256,2048]{1,0:T(8,128)(2,1)}, f32[160,128]{1,0:T(8,128)}, f32[32,128]{1,0:T(8,128)}) custom-call(bf16[256,2048]{1,0:T(8,128)(2,1)} %get-tuple-element.6.c_in, f32[160,128]{1,0:T(8,128)} %get-tuple-element.7.a_in, f32[32,128]{1,0:T(8,128)} %get-tuple-element.8.b_in), custom_call_target="tpu_custom_call" | custom-call | tf_op jit(solution)/shard_map/hand_out/pallas_call | solution.py:721

commit v6 on v5

--- a/solution.py
+++ b/solution.py
@@ -243,6 +243,10 @@
 
     hops = [("node", o) for o in range(1, n_node)] + [("local", o) for o in range(1, n_local)]
 
+    def send_round(j):
+        for axis, o in hops:
+            message(j, axis, o, send.at[j], arr.at[j]).start()
+
     def pack(j, carry):
         for copy in load(j):
             copy.wait()
@@ -260,8 +264,11 @@
         quarters = [stage[j, :, c * GQ : (c + 1) * GQ] for c in range(4)]
         total = dot(pack_hot[...], jnp.concatenate(quarters, axis=0))
         send[j] = total.astype(BF16).reshape(peers, CHUNK, GQ)
-        for axis, o in hops:
-            message(j, axis, o, send.at[j], arr.at[j]).start()
+
+        @pl.when(j < 2)
+        def _():
+            send_round(j)
+
         return carry
 
     lax.fori_loop(0, ROUNDS, pack, 0)
@@ -400,6 +407,11 @@
     def head(r, carry):
         for axis, o in hops:
             arrival(r, axis, o, send.at[r], arr.at[r]).wait_recv()
+
+        @pl.when(r + 2 < ROUNDS)
+        def _():
+            send_round(r + 2)
+
         arrived = arr[r].reshape(entries, GQ)
         per = GQ // HEAD
         for c in range(4):

time: 55.7 us -> 55.1 us (0.989)
  Pallas kernels: 54.9 us -> 54.3 us
where the time goes in v6:
time: 55.1 us; the launch traced here: 55 us
  Pallas kernels  54.3 us (99%)
  between operations  0.64 us (1%)
    pallas_call x1, Pallas kernels, local(): pl.pallas_call(functools.partial(main_kernel, n_local, n_node, factor if...  52.3 us
    pallas_call x1, Pallas kernels, hand_out(): pl.pallas_call(functools.partial(hand_out_kernel, parts), out_shape=tuple...  2.04 us

profile of v6, /device:TPU:0, one launch (start us, length us, event | category | flops | bytes accessed | tf_op | source)
XLA Modules:
  0.0 55.0 jit_solution(18119426197947368481)
XLA Ops:
  0.6 52.3 %exchange_attention.1 = (bf16[256,2048]{1,0:T(8,128)(2,1)}, f32[160,128]{1,0:T(8,128)}, f32[32,128]{1,0:T(8,128)}) custom-call(bf16[256,5120]{1,0:T(8,128)(2,1)} %x_hbm.1, bf16[256,5120]{1,0:T(8,128)(2,1)} %q_hbm.1, bf16[256,2048]{1,0:T(8,128)(2,1)} %kv_hbm.1, bf16[256,5120]{1,0:T(8,128)(2,1)} %g_hbm.1, bf16[5120,128]{1,0:T(8,128)(2,1)} %down_hbm.1, ...), custom_call_target="tpu_custom_call" | custom-call | tf_op jit(solution)/shard_map/exchange_attention/pallas_call | solution.py:777
  52.9 2.0 %hand_out.1 = (bf16[256,2048]{1,0:T(8,128)(2,1)}, f32[160,128]{1,0:T(8,128)}, f32[32,128]{1,0:T(8,128)}) custom-call(bf16[256,2048]{1,0:T(8,128)(2,1)} %get-tuple-element.6.c_in, f32[160,128]{1,0:T(8,128)} %get-tuple-element.7.a_in, f32[32,128]{1,0:T(8,128)} %get-tuple-element.8.b_in), custom_call_target="tpu_custom_call" | custom-call | tf_op jit(solution)/shard_map/hand_out/pallas_call | solution.py:733
